TPU v7x, 32 devices: a whole 2x2x4 slice. The times are simulated.
32 devices in a mesh: lat: 8 (over z, y), lon: 4 (over x, core).
Axes of the slice: x: 2, y: 2, z: 4, core: 2. Of those that a mesh axis runs over, the one named last changes fastest.
Arguments:
- state: float32 [5, 24, 8, 8, 2880], P(None, 'lat', None, None, 'lon'), may hold values from -6 to 6
- courant_x: float32 [24, 8, 8, 2880], P('lat', None, None, 'lon'), may hold values from -4 to 4
- courant_y: float32 [24, 8, 8, 2880], P('lat', None, None, 'lon'), may hold values from -4 to 4
- block_of_slot: int32 [24], P('lat'), may hold values from 0 to 23, as said below
- face_source: int32 [24, 2], P('lat'), may hold values from -1 to 23, as said below
- cutoff: int32 [192], replicated, may hold values from 0 to 256, as said below
Outputs:
- new_state: float32 [5, 24, 8, 8, 2880], P(None, 'lat', None, None, 'lon')
Inputs may be any that keep to these rules, and one draw needn't show every extreme that they name: `block_of_slot`: each block number appears once. The polar blocks are the first and the last 4 block numbers; the 3 slots of one index of lat hold at most 2 polar blocks, and some index holds 2. `face_source`: entry 0 of slot s is the slot holding block block_of_slot[s] - 1 and entry 1 the slot holding block block_of_slot[s] + 1; -1 where that block does not exist. Rows of polar blocks have a cutoff of 1 or more; all other rows have 0.
All inputs are finite; a program needn't handle non-finite values.
Results may differ from a plain program's by a relative error of at most 0.00005.
Values sent between devices are 32-bit elements; how exact they have to be, the bound alone decides.
No kernel may reach another device: no remote copies, remote signals or barrier semaphores. Data moves between devices by JAX's collectives and lax.ppermute only.
A program may use at most 64 MiB of HBM per device.

v0:
```python
import functools
import math

import jax
import jax.numpy as jnp
import numpy as np
from jax import lax
from jax.experimental import pallas as pl
from jax.experimental.pallas import tpu as pltpu
from jax.sharding import PartitionSpec as P

NLON = 2880
KCUT = 256
LANES = 128
VMEM_LIMIT = 50 * 1024 * 1024
BF16 = jnp.bfloat16
F32 = jnp.float32


def phases(columns):
    wavenumber = np.arange(KCUT, dtype=np.int64)
    return (columns[:, None] * wavenumber[None, :] % NLON).astype(np.float64) * (
        2.0 * math.pi / NLON
    )


def basis_tables(width):
    phase = phases(np.arange(width, dtype=np.int64))
    table = np.concatenate([np.cos(phase), np.sin(phase)], axis=1).astype(np.float32)
    high = table.astype(jnp.bfloat16)
    low = (table - high.astype(np.float32)).astype(jnp.bfloat16)
    forward = (jnp.asarray(high), jnp.asarray(low))
    inverse = (
        jnp.asarray(np.ascontiguousarray(high.T)),
        jnp.asarray(np.ascontiguousarray(low.T)),
    )
    return forward, inverse


def turn_table(lon, width):
    phase = phases(np.arange(lon, dtype=np.int64) * width)
    table = np.concatenate([np.cos(phase), np.sin(phase)], axis=1).astype(np.float32)
    return jnp.asarray(table[:, None, :])


def split_dot(rows, high, low):
    rows_high = rows.astype(BF16)
    rows_low = (rows - rows_high.astype(F32)).astype(BF16)
    dot = functools.partial(jnp.dot, preferred_element_type=F32)
    return dot(rows_high, high) + (dot(rows_low, high) + dot(rows_high, low))


def turned(spec, turn, sign):
    real, imag = spec[:, :KCUT], spec[:, KCUT:]
    cos, sin = turn[:, :KCUT], turn[:, KCUT:] * sign
    return jnp.concatenate([real * cos - imag * sin, imag * cos + real * sin], axis=1)


def row_weights(cut):
    column = lax.broadcasted_iota(jnp.int32, (1, 2 * KCUT), 1)
    wavenumber = jnp.where(column >= KCUT, column - KCUT, column)
    scale = jnp.where(wavenumber == 0, 1.0 / NLON, 2.0 / NLON).astype(F32)
    return jnp.where(wavenumber < cut, scale, 0.0)


def pick_slots(block_ref, cutoff_ref, rows):
    polar1 = cutoff_ref[block_ref[1] * rows] > 0
    polar2 = cutoff_ref[block_ref[2] * rows] > 0
    rest = jnp.where(polar2, jnp.where(polar1, 0, 1), 2)
    return jnp.where(rest == 0, 1, 0), jnp.where(rest == 2, 1, 2), rest


def mine_first(pair, core):
    a, b = pair
    return jnp.where(core == 0, a, b), jnp.where(core == 0, b, a)


def vmem(count):
    return [pl.BlockSpec(memory_space=pltpu.VMEM)] * count


def smem(count):
    return [pl.BlockSpec(memory_space=pltpu.SMEM)] * count


def edge_kernel(lane_last, head_ref, tail_ref, wind_ref, west_ref, east_ref):
    fields, slots, rows = head_ref.shape[:3]
    lane = lax.broadcasted_iota(jnp.int32, (8, LANES), 1)
    for s in range(slots):
        west = jnp.zeros((8, LANES), F32)
        east = jnp.zeros((8, LANES), F32)
        for r in range(rows):
            for f in range(fields):
                here = lane == f * rows + r
                west = jnp.where(here, tail_ref[f, s, r, :, lane_last : lane_last + 1], west)
                east = jnp.where(here, head_ref[f, s, r, :, 0:1], east)
            here = lane == fields * rows + r
            west = jnp.where(here, wind_ref[s, r, :, lane_last : lane_last + 1], west)
        west_ref[s] = west
        east_ref[s] = east


def edges(state, courant_x):
    fields, slots, rows, levels, width = state.shape
    last = (width - 1) // LANES
    out = jax.ShapeDtypeStruct((slots, levels, LANES), F32)
    return pl.pallas_call(
        functools.partial(edge_kernel, (width - 1) % LANES),
        grid=(1,),
        in_specs=[
            pl.BlockSpec((fields, slots, rows, levels, LANES), lambda i: (0, 0, 0, 0, 0)),
            pl.BlockSpec((fields, slots, rows, levels, LANES), lambda i: (0, 0, 0, 0, last)),
            pl.BlockSpec((slots, rows, levels, LANES), lambda i: (0, 0, 0, last)),
        ],
        out_specs=[pl.BlockSpec((slots, levels, LANES), lambda i: (0, 0, 0))] * 2,
        out_shape=[out, out],
        cost_estimate=pl.CostEstimate(flops=10**5, bytes_accessed=1200000, transcendentals=0),
        name="edges",
    )(state, state, courant_x)


PIECE = 200


def tile_of(slab, t, width):
    part = slab[:, t * LANES : min((t + 1) * LANES, width)]
    if part.shape[1] < LANES:
        part = jnp.concatenate([part, jnp.zeros((8, LANES - part.shape[1]), F32)], axis=1)
    return part


def pack_kernel(width, first_ref, last_ref, wind_ref, block_ref, out_ref):
    fields, slots = first_ref.shape[:2]
    tiles = -(-width // LANES)

    def put(row, tile):
        out_ref[pl.ds(row, 8, stride=PIECE), :] = tile

    for j in range(slots):
        half = wind_ref[j, 0] * 0.5
        for t in range(tiles):
            row = {0: 192 + 2 * j, 1: 193 + 2 * j, 2: 64 * j + 62, 3: 64 * j + 63}.get(
                t, 64 * j + 26 + t
            )
            put(row, tile_of(half, t, width))
        for f in range(fields):
            north = last_ref[f, j, 0] * half
            south = first_ref[f, j, 0]
            for t in range(tiles):
                put(64 * j + f * tiles + t, tile_of(north, t, width))
                put(64 * j + 32 + f * tiles + t, tile_of(south, t, width))
    lane = lax.broadcasted_iota(jnp.int32, (8, LANES), 1)
    table = jnp.zeros((8, LANES), F32)
    for j in range(slots):
        table = jnp.where(lane == j, block_ref[j].astype(F32), table)
    put(198, table)
    put(199, table)


def pack(state, courant_y, block):
    fields, slots, rows, levels, width = state.shape
    return pl.pallas_call(
        functools.partial(pack_kernel, width),
        grid=(1,),
        in_specs=[
            pl.BlockSpec((fields, slots, 1, levels, width), lambda i: (0, 0, 0, 0, 0)),
            pl.BlockSpec((fields, slots, 1, levels, width), lambda i: (0, 0, rows - 1, 0, 0)),
            pl.BlockSpec((slots, 1, levels, width), lambda i: (0, rows - 1, 0, 0)),
            pl.BlockSpec(memory_space=pltpu.SMEM),
        ],
        out_specs=pl.BlockSpec((levels * PIECE, LANES), lambda i: (0, 0)),
        out_shape=jax.ShapeDtypeStruct((levels * PIECE, LANES), F32),
        cost_estimate=pl.CostEstimate(flops=10**5, bytes_accessed=1700000, transcendentals=0),
        name="pack",
    )(state, state, courant_y, block)


def face_kernel(got_ref, cutoff_ref, pair_ref, rest_ref, face_ref, table_ref, slot_ref, sem):
    parts = got_ref.shape[0]
    slots = face_ref.shape[0] // parts
    count = parts * slots
    copy = pltpu.make_async_copy(got_ref.at[:, 192:200, :], table_ref, sem)
    copy.start()
    copy.wait()
    blocks = [table_ref[s // slots, 6, s % slots].astype(jnp.int32) for s in range(count)]
    slot_ref[0] = -1
    slot_ref[count + 1] = -1
    for s in range(count):
        slot_ref[blocks[s] + 1] = s
    for s in range(count):
        src, j = divmod(s, slots)
        south = slot_ref[blocks[s] + 2]
        safe = jnp.maximum(south, 0)
        from_src = lax.div(safe, slots)
        from_slot = safe - from_src * slots
        half = jnp.concatenate(
            [
                got_ref[src, 192 + 2 * j : 194 + 2 * j, :],
                got_ref[src, 64 * j + 62 : 64 * j + 64, :],
                got_ref[src, 64 * j + 30 : 64 * j + 32, :],
            ],
            axis=0,
        )
        half = jnp.concatenate([half] * 5 + [half[:2]], axis=0)
        other = got_ref[from_src, pl.ds(pl.multiple_of(64 * from_slot + 32, 32), 32), :]
        face = got_ref[src, 64 * j : 64 * j + 32, :] + half * other
        face_ref[s] = jnp.where(south >= 0, face, 0.0)
    for d in range(parts):
        first, second, rest = pick_slots(blocks[slots * d : slots * d + slots], cutoff_ref, 8)
        for slot, out in (
            (first, pair_ref.at[d, 0]),
            (second, pair_ref.at[d, 1]),
            (rest, rest_ref.at[d]),
        ):
            block = jnp.where(
                slot == 0,
                blocks[slots * d],
                jnp.where(slot == 1, blocks[slots * d + 1], blocks[slots * d + 2]),
            )
            north = slot_ref[block]
            out[0] = jnp.where(north >= 0, face_ref[jnp.maximum(north, 0)], 0.0)
            out[1] = face_ref[slots * d + slot]


def faces_of_pieces(got, slots, cutoff):
    parts = got.shape[0]
    return pl.pallas_call(
        face_kernel,
        in_specs=vmem(1) + smem(1),
        out_specs=vmem(2),
        out_shape=[
            jax.ShapeDtypeStruct((parts, 2, 2, 32, LANES), F32),
            jax.ShapeDtypeStruct((parts, 2, 32, LANES), F32),
        ],
        scratch_shapes=[
            pltpu.VMEM((parts * slots, 32, LANES), F32),
            pltpu.SMEM((parts, 8, LANES), F32),
            pltpu.SMEM((parts * slots + 2,), jnp.int32),
            pltpu.SemaphoreType.DMA(()),
        ],
        cost_estimate=pl.CostEstimate(flops=10**5, bytes_accessed=1600000, transcendentals=0),
        name="faces",
    )(got, cutoff)


def to_pieces(units, parts):
    count, levels, width = units.shape
    groups = math.gcd(parts, levels)
    chunks = parts // groups
    span = -(-width // chunks)
    units = jnp.pad(units, ((0, 0), (0, 0), (0, span * chunks - width)))
    units = units.reshape(count, groups, levels // groups, chunks, span)
    return units.transpose(1, 3, 0, 2, 4).reshape(parts, count, levels // groups * span)


def from_pieces(pieces, levels, width):
    parts, count, _ = pieces.shape
    groups = math.gcd(parts, levels)
    chunks = parts // groups
    span = -(-width // chunks)
    pieces = pieces.reshape(groups, chunks, count, levels // groups, span)
    return pieces.transpose(2, 0, 3, 1, 4).reshape(count, levels, chunks * span)[:, :, :width]


def exchange_faces(state, courant_y, face_source):
    fields, slots, rows, levels, width = state.shape
    lat = lax.axis_size("lat")
    count = 2 * fields + 1
    first = state[:, :, 0].transpose(1, 0, 2, 3)
    last = state[:, :, rows - 1].transpose(1, 0, 2, 3)
    half = courant_y[:, rows - 1][:, None] * 0.5
    units = jnp.concatenate([first, last * half, half], axis=1)
    sent = to_pieces(units.reshape(slots * count, levels, width), lat)
    span = sent.shape[2]
    table = jnp.pad(
        face_source.astype(F32).reshape(1, slots * 2), ((0, 0), (0, span - slots * 2))
    )
    sent = jnp.concatenate([sent, jnp.broadcast_to(table[None], (lat, 1, span))], axis=1)
    got = lax.all_to_all(sent, "lat", 0, 0, tiled=True)
    indices = got[:, slots * count, : slots * 2].reshape(lat * slots, 2).astype(jnp.int32)
    data = got[:, : slots * count].reshape(lat * slots, count, span)
    north, south = indices[:, 0], indices[:, 1]
    face = data[:, fields : 2 * fields] + data[:, 2 * fields :] * data[
        jnp.maximum(south, 0), :fields
    ]
    face = jnp.where((south >= 0)[:, None, None], face, 0.0)
    face_north = jnp.where((north >= 0)[:, None, None], face[jnp.maximum(north, 0)], 0.0)
    back = jnp.concatenate([face_north, face], axis=1).reshape(lat, slots * 2 * fields, span)
    back = lax.all_to_all(back, "lat", 0, 0, tiled=True)
    return from_pieces(back, levels, width).reshape(slots, 2, fields, levels, width)


def tendency_kernel(
    state_ref,
    cx_ref,
    cy_ref,
    west_ref,
    east_ref,
    high_ref,
    low_ref,
    turn_ref,
    place_ref,
    block_ref,
    cutoff_ref,
    tend_ref,
    mine_ref,
    other_ref,
):
    fields, slots, rows, levels, width = state_ref.shape

    tiles = -(-width // LANES)
    lane = lax.broadcasted_iota(jnp.int32, (levels, LANES), 1)
    head, tail, last = lane == 0, lane == LANES - 1, lane == (width - 1) % LANES

    def load(ref, *index):
        out = []
        for t in range(tiles):
            part = ref[index + (slice(None), slice(t * LANES, min((t + 1) * LANES, width)))]
            if part.shape[1] < LANES:
                pad = jnp.zeros((levels, LANES - part.shape[1]), F32)
                part = jnp.concatenate([part, pad], axis=1)
            out.append(part)
        return out

    def one_slot(s, carry):
        west, east = west_ref[s], east_ref[s]
        for f in range(fields):
            above = None
            now = load(state_ref, f, s, 0)
            for r in range(rows):
                column = f * rows + r
                left = [pltpu.roll(x, LANES - 1, 1) for x in now]
                left = [
                    jnp.where(tail, left[t + 1], left[t])
                    if t + 1 < tiles
                    else jnp.where(last, east[:, column : column + 1], left[t])
                    for t in range(tiles)
                ]
                half = [x * 0.5 for x in load(cx_ref, s, r)]
                flux = [h * (x + y) for h, x, y in zip(half, now, left)]
                wind = west[:, fields * rows + r : fields * rows + r + 1] * 0.5
                first = wind * (west[:, column : column + 1] + now[0])
                right = [pltpu.roll(x, 1, 1) for x in flux]
                right = [jnp.where(head, y, x) for x, y in zip(right, [first] + right[:-1])]
                change = [x - y for x, y in zip(right, flux)]
                if above is not None:
                    change = [x + y for x, y in zip(change, above)]
                if r + 1 < rows:
                    later = load(state_ref, f, s, r + 1)
                    half = load(cy_ref, s, r)
                    above = [h * 0.5 * (x + y) for h, x, y in zip(half, now, later)]
                    change = [x - y for x, y in zip(change, above)]
                    now = later
                for t in range(tiles):
                    stop = min((t + 1) * LANES, width)
                    tend_ref[f, s, r, :, t * LANES : stop] = change[t][:, : stop - t * LANES]
        return carry

    lax.fori_loop(0, slots, one_slot, 0)
    turn = turn_ref[place_ref[0]]
    first, second, _ = pick_slots(block_ref, cutoff_ref, rows)
    mine, other = mine_first((first, second), place_ref[1])
    for slot, out_ref in ((other, other_ref), (mine, mine_ref)):
        spec = split_dot(
            tend_ref[:, slot].reshape(fields * rows * levels, width), high_ref[...], low_ref[...]
        )
        out_ref[...] = turned(spec, turn, 1.0)


def local_tendency(state, courant_x, courant_y, west, east, forward, turn, place, block, cutoff):
    fields, slots, rows, levels, width = state.shape
    count = fields * rows * levels
    spec = jax.ShapeDtypeStruct((count, 2 * KCUT), F32)
    return pl.pallas_call(
        tendency_kernel,
        in_specs=vmem(8) + smem(3),
        out_specs=vmem(3),
        out_shape=[jax.ShapeDtypeStruct(state.shape, F32), spec, spec],
        compiler_params=pltpu.CompilerParams(vmem_limit_bytes=VMEM_LIMIT),
        cost_estimate=pl.CostEstimate(
            flops=6 * count * 2 * KCUT * width * 2, bytes_accessed=9 * 10**6, transcendentals=0
        ),
        name="tendency",
    )(state, courant_x, courant_y, west, east, *forward, turn, place, block, cutoff)


def main_kernel(
    state_ref,
    tend_ref,
    mine_ref,
    away_ref,
    high_ref,
    low_ref,
    turn_ref,
    place_ref,
    block_ref,
    cutoff_ref,
    out_ref,
    token_ref,
):
    fields, slots, rows, levels, width = state_ref.shape
    token_ref[...] = jnp.zeros_like(token_ref)
    turn = turn_ref[place_ref[0]]
    first, second, rest = pick_slots(block_ref, cutoff_ref, rows)
    mine, other = mine_first((first, second), place_ref[1])
    out_ref[:, rest] = state_ref[:, rest] + tend_ref[:, rest]
    for slot, spec_ref in ((mine, mine_ref), (other, away_ref)):
        spec = turned(spec_ref[...], turn, -1.0).reshape(fields, rows, levels, 2 * KCUT)
        cuts = [cutoff_ref[block_ref[slot] * rows + r] for r in range(rows)]
        spec = jnp.concatenate(
            [spec[:, r : r + 1] * row_weights(cuts[r]) for r in range(rows)], axis=1
        )
        smooth = split_dot(
            spec.reshape(fields * rows * levels, 2 * KCUT), high_ref[...], low_ref[...]
        ).reshape(fields, rows, levels, width)
        for r in range(rows):
            out_ref[:, slot, r] = state_ref[:, slot, r] + jnp.where(
                cuts[r] > 0, smooth[:, r], tend_ref[:, slot, r]
            )


def main_part(state, tend, mine, away, inverse, turn, place, block, cutoff):
    width = state.shape[-1]
    return pl.pallas_call(
        main_kernel,
        in_specs=vmem(7) + smem(3),
        out_specs=vmem(2),
        out_shape=[
            jax.ShapeDtypeStruct(state.shape, F32),
            jax.ShapeDtypeStruct((8, LANES), F32),
        ],
        compiler_params=pltpu.CompilerParams(vmem_limit_bytes=VMEM_LIMIT),
        cost_estimate=pl.CostEstimate(
            flops=12 * mine.shape[0] * 2 * KCUT * width, bytes_accessed=10**7, transcendentals=0
        ),
        name="main",
    )(state, tend, mine, away, *inverse, turn, place, block, cutoff)


def unpack(ref, base, stride, put, fields, width):
    tiles = -(-width // LANES)
    for f in range(fields):
        for t in range(tiles):
            tile = ref[pl.ds(base + f * tiles + t, 8, stride=stride), :]
            stop = min((t + 1) * LANES, width)
            put(f, t * LANES, stop, tile[:, : stop - t * LANES])


def rim_kernel(
    packed,
    token_ref,
    got_ref,
    high_ref,
    low_ref,
    turn_ref,
    place_ref,
    faces_ref,
    mine_ref,
    other_ref,
):
    _, _, fields, levels, width = faces_ref.shape
    if packed:
        for i in range(2):
            for side in range(2):

                def put(f, start, stop, tile, i=i, side=side):
                    faces_ref[i, side, f, :, start:stop] = tile

                unpack(got_ref, 64 * i + 32 * side, 128, put, fields, width)
    else:
        faces_ref[...] = got_ref[...]
    turn = turn_ref[place_ref[0]]
    core = place_ref[1]
    both = jnp.concatenate(
        [part for i in (core, 1 - core) for part in (faces_ref[i, 0], -faces_ref[i, 1])], axis=0
    ).reshape(4 * fields * levels, width)
    spec = turned(split_dot(both, high_ref[...], low_ref[...]), turn, 1.0)
    mine_ref[...] = spec[: 2 * fields * levels]
    other_ref[...] = spec[2 * fields * levels :]


def rim_spectra(token, got, shape, forward, turn, place):
    _, _, fields, levels, width = shape
    spec = jax.ShapeDtypeStruct((2 * fields * levels, 2 * KCUT), F32)
    return pl.pallas_call(
        functools.partial(rim_kernel, got.ndim == 2),
        in_specs=vmem(5) + smem(1),
        out_specs=vmem(3),
        out_shape=[jax.ShapeDtypeStruct(shape, F32), spec, spec],
        compiler_params=pltpu.CompilerParams(vmem_limit_bytes=VMEM_LIMIT),
        cost_estimate=pl.CostEstimate(
            flops=24 * fields * levels * 2 * KCUT * width,
            bytes_accessed=3 * 10**6,
            transcendentals=0,
        ),
        name="rim_spectra",
    )(token, got, *forward, turn, place)


def final_kernel(
    packed,
    main_ref,
    pair_ref,
    back_ref,
    mine_ref,
    away_ref,
    high_ref,
    low_ref,
    turn_ref,
    place_ref,
    block_ref,
    cutoff_ref,
    out_ref,
):
    fields, slots, _, levels, width = main_ref.shape
    rows = 8
    side = pl.program_id(0)
    row = side * (rows - 1)
    turn = turn_ref[place_ref[0]]
    core = place_ref[1]
    first, second, rest = pick_slots(block_ref, cutoff_ref, rows)
    mine, other = mine_first((first, second), core)
    count = fields * levels
    part = pl.ds(pl.multiple_of(side * count, 8), count)
    sign = jnp.where(side == 0, 1.0, -1.0).astype(F32)
    if packed:

        def put(f, start, stop, tile):
            old = main_ref[f, rest, 0, :, start:stop]
            out_ref[f, rest, 0, :, start:stop] = old + tile * sign

        unpack(back_ref, 32 * side, 64, put, fields, width)
    else:
        out_ref[:, rest, 0] = main_ref[:, rest, 0] + back_ref[side] * sign
    cuts = [cutoff_ref[block_ref[slot] * rows + row] for slot in (mine, other)]
    spec = jnp.concatenate(
        [
            turned(ref[part, :], turn, -1.0) * row_weights(cut)
            for ref, cut in ((mine_ref, cuts[0]), (away_ref, cuts[1]))
        ],
        axis=0,
    )
    smooth = split_dot(spec, high_ref[...], low_ref[...]).reshape(2, fields, levels, width)
    for i, (slot, order) in enumerate(((mine, core), (other, 1 - core))):
        out_ref[:, slot, 0] = main_ref[:, slot, 0] + jnp.where(
            cuts[i] > 0, smooth[i], pair_ref[order, side] * sign
        )


def final_part(main, pair, back, mine, away, inverse, turn, place, block, cutoff):
    fields, slots, rows, levels, width = main.shape
    block_spec = pl.BlockSpec(
        (fields, slots, 1, levels, width), lambda i: (0, 0, i * (rows - 1), 0, 0)
    )
    return pl.pallas_call(
        functools.partial(final_kernel, back.ndim == 2),
        grid=(2,),
        in_specs=[block_spec] + vmem(7) + smem(3),
        out_specs=block_spec,
        out_shape=jax.ShapeDtypeStruct(main.shape, F32),
        input_output_aliases={0: 0},
        compiler_params=pltpu.CompilerParams(vmem_limit_bytes=VMEM_LIMIT),
        cost_estimate=pl.CostEstimate(
            flops=12 * mine.shape[0] * 2 * KCUT * width,
            bytes_accessed=4 * 10**6,
            transcendentals=0,
        ),
        name="final",
    )(main, pair, back, mine, away, *inverse, turn, place, block, cutoff)


def swap(array, bit):
    size = lax.axis_size("lon")
    return lax.ppermute(array, "lon", [(i, i ^ bit) for i in range(size)])


def lon_sum(mine, other):
    total = mine + swap(other, 1)
    bit = 2
    while bit < lax.axis_size("lon"):
        total = total + swap(total, bit)
        bit *= 2
    return total, swap(total, 1)


def shards(state, courant_x, courant_y, block_of_slot, face_source, cutoff):
    fields, slots, rows, levels, width = state.shape
    lat, lon = lax.axis_size("lat"), lax.axis_size("lon")
    lon_index = lax.axis_index("lon")
    place = jnp.stack([lon_index, lon_index % 2]).astype(jnp.int32)
    forward, inverse = basis_tables(width)
    turn = turn_table(lon, width)
    tables = (turn, place, block_of_slot, cutoff)

    packed = lat == levels == 8 and -(-width // LANES) * fields == 30
    if packed:
        sent = pack(state, courant_y, block_of_slot).reshape(lat, PIECE, LANES)
        got = lax.all_to_all(sent, "lat", 0, 0, tiled=True)

    west, east = edges(state, courant_x)
    west = lax.ppermute(west, "lon", [(i, (i + 1) % lon) for i in range(lon)])
    east = lax.ppermute(east, "lon", [((i + 1) % lon, i) for i in range(lon)])
    tend, mine, other = local_tendency(
        state, courant_x, courant_y, west, east, forward, *tables
    )
    total, away = lon_sum(mine, other)
    main, token = main_part(state, tend, total, away, inverse, *tables)

    if packed:
        pair, rest = faces_of_pieces(got, slots, cutoff)
        pair, rest = (
            lax.all_to_all(x.reshape(lat, -1, LANES), "lat", 0, 0, tiled=True).reshape(-1, LANES)
            for x in (pair, rest)
        )
    else:
        faces = exchange_faces(state, courant_y, face_source)
        picked = pick_slots(block_of_slot, cutoff, rows)
        pair, rest = faces[jnp.stack(picked[:2])], faces[picked[2]]
    shape = (2, 2, fields, levels, width)
    pair, rim_mine, rim_other = rim_spectra(token, pair, shape, forward, turn, place)
    rim_total, rim_away = lon_sum(rim_mine, rim_other)
    return final_part(main, pair, rest, rim_total, rim_away, inverse, *tables)


def solution(mesh):
    placed = (
        P(None, "lat", None, None, "lon"),
        P("lat", None, None, "lon"),
        P("lat", None, None, "lon"),
        P("lat"),
        P("lat", None),
        P(),
    )
    return jax.shard_map(
        shards,
        mesh=mesh,
        in_specs=placed,
        out_specs=P(None, "lat", None, None, "lon"),
        check_vma=False,
    )
```

profile of v0, /device:TPU:0, one launch (start us, length us, event | category | flops | bytes accessed | tf_op | source)
XLA Modules:
  0.0 82.3 jit_solution(6271862243677569542)
XLA Ops:
  0.0 2.1 %pack.1 = f32[1600,128]{1,0:T(8,128)} custom-call(f32[5,3,8,8,720]{4,3,2,1,0:T(8,128)} %last_ref.1, f32[5,3,8,8,720]{4,3,2,1,0:T(8,128)} %last_ref.1, f32[3,8,8,720]{3,2,1,0:T(8,128)} %wind_ref.3, s32[3]{0:T(128)} %block_ref.7), custom_call_target="tpu_custom_call" | custom-call | flops 100000 | bytes 1700000 | tf_op jit(solution)/shard_map/pack/pallas_call | solution.py:162
  2.1 7.3 %all-to-all-start = ((f32[8,200,128]{2,1,0:T(8,128)}), f32[8,200,128]{2,1,0:T(8,128)}, u32[]{:S(2)}, u32[]{:S(2)}) async-start(f32[8,200,128]{2,1,0:T(8,128)} %bitcast.8), calls=%async_computation | async-start | bytes 1638400 | tf_op jit(solution)/shard_map/all_to_all | solution.py:598
  9.5 2.4 %edges.1 = (f32[3,8,128]{2,1,0:T(8,128)}, f32[3,8,128]{2,1,0:T(8,128)}) custom-call(f32[5,3,8,8,720]{4,3,2,1,0:T(8,128)} %last_ref.1, f32[5,3,8,8,720]{4,3,2,1,0:T(8,128)} %last_ref.1, f32[3,8,8,720]{3,2,1,0:T(8,128)} %cx_ref.1), custom_call_target="tpu_custom_call" | custom-call | flops 100000 | bytes 1200000 | tf_op jit(solution)/shard_map/edges/pallas_call | solution.py:107
  11.9 1.7 %collective-permute-start.1 = (f32[3,8,128]{2,1,0:T(8,128)}, f32[3,8,128]{2,1,0:T(8,128)S(1)}, u32[]{:S(2)}, u32[]{:S(2)}) collective-permute-start(f32[3,8,128]{2,1,0:T(8,128)} %get-tuple-element.18), channel_id=1, source_target_pairs={{1,0},{2,1},{3,2},{0,3},{5,4},{6,5},{7,6},{4,7},{9,8},{10,9},{11,1... | collective-permute-start | bytes 36872 | tf_op jit(solution)/shard_map/ppermute | solution.py:602
  13.6 0.1 pad_add_fusion.place_ref
  13.7 1.5 %collective-permute-done.west_ref = f32[3,8,128]{2,1,0:T(8,128)S(1)} collective-permute-done((f32[3,8,128]{2,1,0:T(8,128)}, f32[3,8,128]{2,1,0:T(8,128)S(1)}, u32[]{:S(2)}, u32[]{:S(2)}) %collective-permute-start) | collective-permute-done | bytes 12320 | tf_op jit(solution)/shard_map/ppermute | solution.py:601
  15.2 0.0 collective-permute-done.1.east_ref
  15.3 11.7 %tendency.1 = (f32[5,3,8,8,720]{4,3,2,1,0:T(8,128)}, f32[320,512]{1,0:T(8,128)S(1)}, f32[320,512]{1,0:T(8,128)S(1)}) custom-call(f32[5,3,8,8,720]{4,3,2,1,0:T(8,128)} %last_ref.1, f32[3,8,8,720]{3,2,1,0:T(8,128)S(1)} %copy-done.4, f32[3,8,8,720]{3,2,1,0:T(8,128)S(1)} %copy-done.5, f32[3,8,128]{2,1,0:T(8,128)S(1)} %collective-permute-done.west_ref, ...), custom_call_target="tpu_custom_call" | custom-call | flops 1415577600 | bytes 9000000 | tf_op jit(solution)/shard_map/tendency/pallas_call | solution.py:374
  27.0 2.0 %collective-permute-start.2 = (f32[320,512]{1,0:T(8,128)S(1)}, f32[320,512]{1,0:T(8,128)S(1)}, u32[]{:S(2)}, u32[]{:S(2)}) collective-permute-start(f32[320,512]{1,0:T(8,128)S(1)} %get-tuple-element.21), channel_id=1, source_target_pairs={{0,1},{1,0},{2,3},{3,2},{4,5},{5,4},{6,7},{7,6},{8,9},{9,8},{10,11... | collective-permute-start | bytes 1966088 | tf_op jit(solution)/shard_map/ppermute | solution.py:574
  29.1 1.7 %collective-permute-done.2 = f32[320,512]{1,0:T(8,128)S(1)} collective-permute-done((f32[320,512]{1,0:T(8,128)S(1)}, f32[320,512]{1,0:T(8,128)S(1)}, u32[]{:S(2)}, u32[]{:S(2)}) %collective-permute-start.2) | collective-permute-done | bytes 655392 | tf_op jit(solution)/shard_map/ppermute | solution.py:574
  30.8 1.0 %add.17 = f32[320,512]{1,0:T(8,128)} add(f32[320,512]{1,0:T(8,128)S(1)} %get-tuple-element.20, f32[320,512]{1,0:T(8,128)S(1)} %collective-permute-done.2) | non-fusion elementwise | flops 163840 | bytes 1966080 | tf_op jit(solution)/shard_map/add | solution.py:578
  31.7 0.5 collective-permute-start.3
  32.3 3.4 %faces.1 = (f32[8,2,2,32,128]{4,3,2,1,0:T(8,128)}, f32[8,2,32,128]{3,2,1,0:T(8,128)}) custom-call(f32[8,200,128]{2,1,0:T(8,128)} %all-to-all-done.got_ref, s32[192]{0:T(256)} %cutoff_ref.7), custom_call_target="tpu_custom_call" | custom-call | flops 100000 | bytes 1600000 | tf_op jit(solution)/shard_map/faces/pallas_call | solution.py:227
  35.7 6.0 %all-to-all-start.1 = ((f32[8,128,128]{2,1,0:T(8,128)}), f32[8,128,128]{2,1,0:T(8,128)}, u32[]{:S(2)}, u32[]{:S(2)}) async-start(f32[8,128,128]{2,1,0:T(8,128)} %bitcast.9), calls=%async_computation.1 | async-start | bytes 1048576 | tf_op jit(solution)/shard_map/all_to_all | solution.py:612
  41.7 7.3 %collective-permute-done.3 = f32[320,512]{1,0:T(8,128)} collective-permute-done((f32[320,512]{1,0:T(8,128)}, f32[320,512]{1,0:T(8,128)}, u32[]{:S(2)}, u32[]{:S(2)}) %collective-permute-start.3) | collective-permute-done | bytes 655392 | tf_op jit(solution)/shard_map/ppermute | solution.py:574
  49.1 1.4 %add.18.mine_ref = f32[320,512]{1,0:T(8,128)S(1)} add(f32[320,512]{1,0:T(8,128)} %add.17, f32[320,512]{1,0:T(8,128)} %collective-permute-done.3) | non-fusion elementwise | flops 163840 | bytes 1966080 | tf_op jit(solution)/shard_map/add | solution.py:581
  50.5 0.1 collective-permute-start.4
  50.5 2.1 %collective-permute-done.4.away_ref = f32[320,512]{1,0:T(8,128)S(1)} collective-permute-done((f32[320,512]{1,0:T(8,128)S(1)}, f32[320,512]{1,0:T(8,128)S(1)}, u32[]{:S(2)}, u32[]{:S(2)}) %collective-permute-start.4) | collective-permute-done | bytes 655392 | tf_op jit(solution)/shard_map/ppermute | solution.py:574
  52.6 6.1 %main.1 = (f32[5,3,8,8,720]{4,3,2,1,0:T(8,128)}, f32[8,128]{1,0:T(8,128)S(1)}) custom-call(f32[5,3,8,8,720]{4,3,2,1,0:T(8,128)} %last_ref.1, f32[5,3,8,8,720]{4,3,2,1,0:T(8,128)} %get-tuple-element.19.tend_ref, f32[320,512]{1,0:T(8,128)S(1)} %add.18.mine_ref, f32[320,512]{1,0:T(8,128)S(1)} %collective-permute-done.4.away_ref, bf16[512,720]{1,0:T(8,128)(2,1)S(1)} %copy-done, ...), custom_call_target="tpu_custom_call" | custom-call | flops 1415577600 | bytes 10000000 | tf_op jit(solution)/shard_map/main/pallas_call | solution.py:424
  58.8 0.6 copy-done.12
  59.4 0.7 copy-done.13
  60.0 2.6 %rim_spectra.1 = (f32[2,2,5,8,720]{4,3,2,1,0:T(8,128)S(1)}, f32[80,512]{1,0:T(8,128)S(1)}, f32[80,512]{1,0:T(8,128)}) custom-call(f32[8,128]{1,0:T(8,128)S(1)} %copy-done.13, f32[1024,128]{1,0:T(8,128)} %bitcast.4.got_ref, bf16[720,512]{1,0:T(8,128)(2,1)S(1)} %copy-done.2, bf16[720,512]{1,0:T(8,128)(2,1)S(1)} %copy-done.3, f32[4,1,512]{2,1,0:T(1,128)S(1)} %copy-done.7, ...), custom_call_target="tpu_custom_call" | custom-call | flops 353894400 | bytes 3000000 | tf_op jit(solution)/shard_map/rim_spectra/pallas_call | solution.py:485
  62.6 0.7 copy-done.6
  63.3 0.1 collective-permute-start.5
  63.4 6.0 %all-to-all-start.2 = ((f32[8,64,128]{2,1,0:T(8,128)}), f32[8,64,128]{2,1,0:T(8,128)S(1)}, u32[]{:S(2)}, u32[]{:S(2)}) async-start(f32[8,64,128]{2,1,0:T(8,128)} %bitcast.10), calls=%async_computation.2 | async-start | bytes 524288 | tf_op jit(solution)/shard_map/all_to_all | solution.py:612
  69.4 0.9 %add.19 = f32[80,512]{1,0:T(8,128)S(1)} add(f32[80,512]{1,0:T(8,128)} %copy-done.6, f32[80,512]{1,0:T(8,128)S(1)} %collective-permute-done.5) | non-fusion elementwise | flops 40960 | bytes 491520 | tf_op jit(solution)/shard_map/add | solution.py:578
  70.3 0.6 collective-permute-start.6
  70.9 5.7 %collective-permute-done.6 = f32[80,512]{1,0:T(8,128)S(1)} collective-permute-done((f32[80,512]{1,0:T(8,128)S(1)}, f32[80,512]{1,0:T(8,128)S(1)}, u32[]{:S(2)}, u32[]{:S(2)}) %collective-permute-start.6) | collective-permute-done | bytes 163872 | tf_op jit(solution)/shard_map/ppermute | solution.py:574
  76.6 0.1 collective-permute-start.7
  76.7 2.1 %all-to-all-done.2 = f32[8,64,128]{2,1,0:T(8,128)S(1)} async-done(((f32[8,64,128]{2,1,0:T(8,128)}), f32[8,64,128]{2,1,0:T(8,128)S(1)}, u32[]{:S(2)}, u32[]{:S(2)}) %all-to-all-start.2) | async-done | bytes 262176 | tf_op jit(solution)/shard_map/all_to_all | solution.py:612
  78.8 0.7 copy-done.11
  79.5 2.8 %final.1 = f32[5,3,8,8,720]{4,3,2,1,0:T(8,128)} custom-call(f32[5,3,8,8,720]{4,3,2,1,0:T(8,128)} %get-tuple-element.22.main_ref, f32[2,2,5,8,720]{4,3,2,1,0:T(8,128)S(1)} %get-tuple-element.25.pair_ref, f32[512,128]{1,0:T(8,128)S(1)} %bitcast.7, f32[80,512]{1,0:T(8,128)S(1)} %add.20.mine_ref, ...), custom_call_target="tpu_custom_call", output_to_operand_aliasing={{}: (0, {})} | custom-call | flops 353894400 | bytes 4000000 | tf_op jit(solution)/shard_map/final/pallas_call | solution.py:555
  (30 shorter events, 0.1 us)
Async XLA Ops:
  2.1 30.2 %all-to-all-start = ((f32[8,200,128]{2,1,0:T(8,128)}), f32[8,200,128]{2,1,0:T(8,128)}, u32[]{:S(2)}, u32[]{:S(2)}) async-start(f32[8,200,128]{2,1,0:T(8,128)} %bitcast.8), calls=%async_computation | async-start | bytes 1638400 | tf_op jit(solution)/shard_map/all_to_all | solution.py:598
  9.4 5.8 %copy-start.2 = (bf16[720,512]{1,0:T(8,128)(2,1)S(1)}, bf16[720,512]{1,0:T(8,128)(2,1)}, u32[]{:S(2)}) copy-start(bf16[720,512]{1,0:T(8,128)(2,1)} %constant.27.clone.high_ref) | copy-start | bytes 2211844
  9.4 5.8 %copy-start.3 = (bf16[720,512]{1,0:T(8,128)(2,1)S(1)}, bf16[720,512]{1,0:T(8,128)(2,1)}, u32[]{:S(2)}) copy-start(bf16[720,512]{1,0:T(8,128)(2,1)} %constant.28.clone.low_ref) | copy-start | bytes 2211844
  9.4 5.8 %copy-start.4 = (f32[3,8,8,720]{3,2,1,0:T(8,128)S(1)}, f32[3,8,8,720]{3,2,1,0:T(8,128)}, u32[]{:S(2)}) copy-start(f32[3,8,8,720]{3,2,1,0:T(8,128)} %cx_ref.1) | copy-start | bytes 1658884
  9.4 5.8 %copy-start.5 = (f32[3,8,8,720]{3,2,1,0:T(8,128)S(1)}, f32[3,8,8,720]{3,2,1,0:T(8,128)}, u32[]{:S(2)}) copy-start(f32[3,8,8,720]{3,2,1,0:T(8,128)} %wind_ref.3) | copy-start | bytes 1658884
  9.5 5.8 %copy-start.7 = (f32[4,1,512]{2,1,0:T(1,128)S(1)}, f32[4,1,512]{2,1,0:T(1,128)}, u32[]{:S(2)}) copy-start(f32[4,1,512]{2,1,0:T(1,128)} %constant.31.clone.turn_ref) | copy-start | bytes 24580
  9.5 5.8 %copy-start.8 = (s32[192]{0:T(256)S(1)}, s32[192]{0:T(256)}, u32[]{:S(2)}) copy-start(s32[192]{0:T(256)} %cutoff_ref.7) | copy-start | bytes 2308
  9.5 5.8 %copy-start.10 = (s32[3]{0:T(128)S(1)}, s32[3]{0:T(128)}, u32[]{:S(2)}) copy-start(s32[3]{0:T(128)} %block_ref.7) | copy-start | bytes 40
  11.9 3.3 %collective-permute-start = (f32[3,8,128]{2,1,0:T(8,128)}, f32[3,8,128]{2,1,0:T(8,128)S(1)}, u32[]{:S(2)}, u32[]{:S(2)}) collective-permute-start(f32[3,8,128]{2,1,0:T(8,128)} %get-tuple-element.17), channel_id=1, source_target_pairs={{0,1},{1,2},{2,3},{3,0},{4,5},{5,6},{6,7},{7,4},{8,9},{9,10},{10,1... | collective-permute-start | bytes 36872 | tf_op jit(solution)/shard_map/ppermute | solution.py:601
  11.9 3.4 %collective-permute-start.1 = (f32[3,8,128]{2,1,0:T(8,128)}, f32[3,8,128]{2,1,0:T(8,128)S(1)}, u32[]{:S(2)}, u32[]{:S(2)}) collective-permute-start(f32[3,8,128]{2,1,0:T(8,128)} %get-tuple-element.18), channel_id=1, source_target_pairs={{1,0},{2,1},{3,2},{0,3},{5,4},{6,5},{7,6},{4,7},{9,8},{10,9},{11,1... | collective-permute-start | bytes 36872 | tf_op jit(solution)/shard_map/ppermute | solution.py:602
  27.0 25.7 %copy-start = (bf16[512,720]{1,0:T(8,128)(2,1)S(1)}, bf16[512,720]{1,0:T(8,128)(2,1)}, u32[]{:S(2)}) copy-start(bf16[512,720]{1,0:T(8,128)(2,1)} %constant.29.clone.high_ref) | copy-start | bytes 2211844
  27.0 25.7 %copy-start.1 = (bf16[512,720]{1,0:T(8,128)(2,1)S(1)}, bf16[512,720]{1,0:T(8,128)(2,1)}, u32[]{:S(2)}) copy-start(bf16[512,720]{1,0:T(8,128)(2,1)} %constant.30.clone.low_ref) | copy-start | bytes 2211844
  27.0 25.6 %copy-start.9 = (s32[192]{0:T(256)S(1)}, s32[192]{0:T(256)}, u32[]{:S(2)}) copy-start(s32[192]{0:T(256)} %cutoff_ref.7) | copy-start | bytes 2308
  27.0 3.8 %collective-permute-start.2 = (f32[320,512]{1,0:T(8,128)S(1)}, f32[320,512]{1,0:T(8,128)S(1)}, u32[]{:S(2)}, u32[]{:S(2)}) collective-permute-start(f32[320,512]{1,0:T(8,128)S(1)} %get-tuple-element.21), channel_id=1, source_target_pairs={{0,1},{1,0},{2,3},{3,2},{4,5},{5,4},{6,7},{7,6},{8,9},{9,8},{10,11... | collective-permute-start | bytes 1966088 | tf_op jit(solution)/shard_map/ppermute | solution.py:574
  31.7 17.3 %collective-permute-start.3 = (f32[320,512]{1,0:T(8,128)}, f32[320,512]{1,0:T(8,128)}, u32[]{:S(2)}, u32[]{:S(2)}) collective-permute-start(f32[320,512]{1,0:T(8,128)} %add.17), channel_id=1, source_target_pairs={{0,2},{1,3},{2,0},{3,1},{4,6},{5,7},{6,4},{7,5},{8,10},{9,11},{10,... | collective-permute-start | bytes 1966088 | tf_op jit(solution)/shard_map/ppermute | solution.py:574
  35.7 23.6 %all-to-all-start.1 = ((f32[8,128,128]{2,1,0:T(8,128)}), f32[8,128,128]{2,1,0:T(8,128)}, u32[]{:S(2)}, u32[]{:S(2)}) async-start(f32[8,128,128]{2,1,0:T(8,128)} %bitcast.9), calls=%async_computation.1 | async-start | bytes 1048576 | tf_op jit(solution)/shard_map/all_to_all | solution.py:612
  50.5 2.2 %collective-permute-start.4 = (f32[320,512]{1,0:T(8,128)S(1)}, f32[320,512]{1,0:T(8,128)S(1)}, u32[]{:S(2)}, u32[]{:S(2)}) collective-permute-start(f32[320,512]{1,0:T(8,128)S(1)} %add.18.mine_ref), channel_id=1, source_target_pairs={{0,1},{1,0},{2,3},{3,2},{4,5},{5,4},{6,7},{7,6},{8,9},{9,8},{10,11... | collective-permute-start | bytes 1966088 | tf_op jit(solution)/shard_map/ppermute | solution.py:574
  58.8 0.6 copy-start.12
  59.4 0.7 copy-start.13
  62.6 0.7 copy-start.6
  63.3 6.1 %collective-permute-start.5 = (f32[80,512]{1,0:T(8,128)}, f32[80,512]{1,0:T(8,128)S(1)}, u32[]{:S(2)}, u32[]{:S(2)}) collective-permute-start(f32[80,512]{1,0:T(8,128)} %get-tuple-element.28), channel_id=1, source_target_pairs={{0,1},{1,0},{2,3},{3,2},{4,5},{5,4},{6,7},{7,6},{8,9},{9,8},{10,11... | collective-permute-start | bytes 491528 | tf_op jit(solution)/shard_map/ppermute | solution.py:574
  63.4 15.4 %all-to-all-start.2 = ((f32[8,64,128]{2,1,0:T(8,128)}), f32[8,64,128]{2,1,0:T(8,128)S(1)}, u32[]{:S(2)}, u32[]{:S(2)}) async-start(f32[8,64,128]{2,1,0:T(8,128)} %bitcast.10), calls=%async_computation.2 | async-start | bytes 524288 | tf_op jit(solution)/shard_map/all_to_all | solution.py:612
  70.3 6.3 %collective-permute-start.6 = (f32[80,512]{1,0:T(8,128)S(1)}, f32[80,512]{1,0:T(8,128)S(1)}, u32[]{:S(2)}, u32[]{:S(2)}) collective-permute-start(f32[80,512]{1,0:T(8,128)S(1)} %add.19), channel_id=1, source_target_pairs={{0,2},{1,3},{2,0},{3,1},{4,6},{5,7},{6,4},{7,5},{8,10},{9,11},{10,... | collective-permute-start | bytes 491528 | tf_op jit(solution)/shard_map/ppermute | solution.py:574
  76.6 2.2 %collective-permute-start.7 = (f32[80,512]{1,0:T(8,128)S(1)}, f32[80,512]{1,0:T(8,128)S(1)}, u32[]{:S(2)}, u32[]{:S(2)}) collective-permute-start(f32[80,512]{1,0:T(8,128)S(1)} %add.20.mine_ref), channel_id=1, source_target_pairs={{0,1},{1,0},{2,3},{3,2},{4,5},{5,4},{6,7},{7,6},{8,9},{9,8},{10,11... | collective-permute-start | bytes 491528 | tf_op jit(solution)/shard_map/ppermute | solution.py:574
  78.8 0.7 copy-start.11
where the time goes:
time: 82.9 us; the launch traced here: 82.3 us
  Pallas kernels  31.2 us (38%)
  starting transfers between devices  24.5 us (30%)
  waiting for transfers between devices  20.5 us (25%)
  other arithmetic  3.39 us (4%)
  local copies, waits for them, and re-layouts  2.65 us (3%)
    ppermute x6, waiting for transfers between devices, swap(): return lax.ppermute(array, 'lon', [(i, i ^ bit) for i in range(size)])  16.8 us
    all_to_all x2, starting transfers between devices, shards(): lax.all_to_all(x.reshape(lat, -1, LANES), 'lat', 0, 0, tiled=True)  12 us
    pallas_call x1, Pallas kernels, local_tendency(): pl.pallas_call(tendency_kernel, in_specs=vmem(8) + smem(3), out_specs=vme...  11.7 us
    all_to_all x1, starting transfers between devices, shards(): got = lax.all_to_all(sent, 'lat', 0, 0, tiled=True)  7.28 us
    pallas_call x1, Pallas kernels, main_part(): pl.pallas_call(main_kernel, in_specs=vmem(7) + smem(3), out_specs=vmem(2)...  6.12 us
    ppermute x6, starting transfers between devices, swap(): return lax.ppermute(array, 'lon', [(i, i ^ bit) for i in range(size)])  3.47 us
    pallas_call x1, Pallas kernels, faces_of_pieces(): pl.pallas_call(face_kernel, in_specs=vmem(1) + smem(1), out_specs=vmem(2)...  3.44 us
    pallas_call x1, Pallas kernels, final_part(): pl.pallas_call(functools.partial(final_kernel, back.ndim == 2), grid=(2,)...  2.83 us
  transfers between devices with their start and end apart: 11, of which 6 were waited for; matrix products, arithmetic and copies ran while one was open for 4% of the time, Pallas kernels for 29%

commit v1 on v0

--- a/solution.py
+++ b/solution.py
@@ -120,6 +120,7 @@
 
 
 PIECE = 200
+BACK = 192
 
 
 def tile_of(slab, t, width):
@@ -175,7 +176,7 @@
     )(state, state, courant_y, block)
 
 
-def face_kernel(got_ref, cutoff_ref, pair_ref, rest_ref, face_ref, table_ref, slot_ref, sem):
+def face_kernel(got_ref, cutoff_ref, out_ref, face_ref, table_ref, slot_ref, sem):
     parts = got_ref.shape[0]
     slots = face_ref.shape[0] // parts
     count = parts * slots
@@ -207,11 +208,8 @@
         face_ref[s] = jnp.where(south >= 0, face, 0.0)
     for d in range(parts):
         first, second, rest = pick_slots(blocks[slots * d : slots * d + slots], cutoff_ref, 8)
-        for slot, out in (
-            (first, pair_ref.at[d, 0]),
-            (second, pair_ref.at[d, 1]),
-            (rest, rest_ref.at[d]),
-        ):
+        for i, slot in enumerate((first, second, rest)):
+            out = out_ref.at[d, i]
             block = jnp.where(
                 slot == 0,
                 blocks[slots * d],
@@ -227,11 +225,8 @@
     return pl.pallas_call(
         face_kernel,
         in_specs=vmem(1) + smem(1),
-        out_specs=vmem(2),
-        out_shape=[
-            jax.ShapeDtypeStruct((parts, 2, 2, 32, LANES), F32),
-            jax.ShapeDtypeStruct((parts, 2, 32, LANES), F32),
-        ],
+        out_specs=vmem(1)[0],
+        out_shape=jax.ShapeDtypeStruct((parts, slots, 2, 32, LANES), F32),
         scratch_shapes=[
             pltpu.VMEM((parts * slots, 32, LANES), F32),
             pltpu.SMEM((parts, 8, LANES), F32),
@@ -302,11 +297,18 @@
     place_ref,
     block_ref,
     cutoff_ref,
-    tend_ref,
+    out_ref,
     mine_ref,
     other_ref,
+    tend_ref,
+    base_ref,
+    sem,
 ):
     fields, slots, rows, levels, width = state_ref.shape
+
+    def streamed(s):
+        return pltpu.make_async_copy(base_ref.at[:, s], out_ref.at[:, s], sem.at[s])
+
 
     tiles = -(-width // LANES)
     lane = lax.broadcasted_iota(jnp.int32, (levels, LANES), 1)
@@ -350,21 +352,26 @@
                     half = load(cy_ref, s, r)
                     above = [h * 0.5 * (x + y) for h, x, y in zip(half, now, later)]
                     change = [x - y for x, y in zip(change, above)]
-                    now = later
                 for t in range(tiles):
                     stop = min((t + 1) * LANES, width)
+                    base = now[t] + change[t]
                     tend_ref[f, s, r, :, t * LANES : stop] = change[t][:, : stop - t * LANES]
+                    base_ref[f, s, r, :, t * LANES : stop] = base[:, : stop - t * LANES]
+                now = later
+        streamed(s).start()
         return carry
 
     lax.fori_loop(0, slots, one_slot, 0)
     turn = turn_ref[place_ref[0]]
     first, second, _ = pick_slots(block_ref, cutoff_ref, rows)
     mine, other = mine_first((first, second), place_ref[1])
-    for slot, out_ref in ((other, other_ref), (mine, mine_ref)):
+    for slot, spec_ref in ((other, other_ref), (mine, mine_ref)):
         spec = split_dot(
             tend_ref[:, slot].reshape(fields * rows * levels, width), high_ref[...], low_ref[...]
         )
-        out_ref[...] = turned(spec, turn, 1.0)
+        spec_ref[...] = turned(spec, turn, 1.0)
+    for s in range(slots):
+        streamed(s).wait()
 
 
 def local_tendency(state, courant_x, courant_y, west, east, forward, turn, place, block, cutoff):
@@ -374,8 +381,13 @@
     return pl.pallas_call(
         tendency_kernel,
         in_specs=vmem(8) + smem(3),
-        out_specs=vmem(3),
+        out_specs=[pl.BlockSpec(memory_space=pl.ANY)] + vmem(2),
         out_shape=[jax.ShapeDtypeStruct(state.shape, F32), spec, spec],
+        scratch_shapes=[
+            pltpu.VMEM(state.shape, F32),
+            pltpu.VMEM(state.shape, F32),
+            pltpu.SemaphoreType.DMA((slots,)),
+        ],
         compiler_params=pltpu.CompilerParams(vmem_limit_bytes=VMEM_LIMIT),
         cost_estimate=pl.CostEstimate(
             flops=6 * count * 2 * KCUT * width * 2, bytes_accessed=9 * 10**6, transcendentals=0
@@ -384,57 +396,72 @@
     )(state, courant_x, courant_y, west, east, *forward, turn, place, block, cutoff)
 
 
+def chosen_slot(i, place_ref, block_ref, cutoff_ref, rows):
+    first, second, _ = pick_slots(block_ref, cutoff_ref, rows)
+    return jnp.where(i == place_ref[1], first, second)
+
+
 def main_kernel(
+    place_ref,
+    block_ref,
+    cutoff_ref,
     state_ref,
-    tend_ref,
+    base_ref,
     mine_ref,
     away_ref,
     high_ref,
     low_ref,
     turn_ref,
-    place_ref,
-    block_ref,
-    cutoff_ref,
     out_ref,
     token_ref,
 ):
-    fields, slots, rows, levels, width = state_ref.shape
+    fields, _, rows, levels, width = state_ref.shape
     token_ref[...] = jnp.zeros_like(token_ref)
+    i = pl.program_id(0)
     turn = turn_ref[place_ref[0]]
-    first, second, rest = pick_slots(block_ref, cutoff_ref, rows)
-    mine, other = mine_first((first, second), place_ref[1])
-    out_ref[:, rest] = state_ref[:, rest] + tend_ref[:, rest]
-    for slot, spec_ref in ((mine, mine_ref), (other, away_ref)):
-        spec = turned(spec_ref[...], turn, -1.0).reshape(fields, rows, levels, 2 * KCUT)
-        cuts = [cutoff_ref[block_ref[slot] * rows + r] for r in range(rows)]
-        spec = jnp.concatenate(
-            [spec[:, r : r + 1] * row_weights(cuts[r]) for r in range(rows)], axis=1
+    slot = chosen_slot(i, place_ref, block_ref, cutoff_ref, rows)
+    spec = turned(jnp.where(i == 0, mine_ref[...], away_ref[...]), turn, -1.0)
+    spec = spec.reshape(fields, rows, levels, 2 * KCUT)
+    cuts = [cutoff_ref[block_ref[slot] * rows + r] for r in range(rows)]
+    spec = jnp.concatenate(
+        [spec[:, r : r + 1] * row_weights(cuts[r]) for r in range(rows)], axis=1
+    )
+    smooth = split_dot(
+        spec.reshape(fields * rows * levels, 2 * KCUT), high_ref[...], low_ref[...]
+    ).reshape(fields, rows, levels, width)
+    for r in range(rows):
+        out_ref[:, 0, r] = jnp.where(
+            cuts[r] > 0, state_ref[:, 0, r] + smooth[:, r], base_ref[:, 0, r]
         )
-        smooth = split_dot(
-            spec.reshape(fields * rows * levels, 2 * KCUT), high_ref[...], low_ref[...]
-        ).reshape(fields, rows, levels, width)
-        for r in range(rows):
-            out_ref[:, slot, r] = state_ref[:, slot, r] + jnp.where(
-                cuts[r] > 0, smooth[:, r], tend_ref[:, slot, r]
-            )
-
-
-def main_part(state, tend, mine, away, inverse, turn, place, block, cutoff):
-    width = state.shape[-1]
+
+
+def main_part(state, base, mine, away, inverse, turn, place, block, cutoff):
+    fields, slots, rows, levels, width = state.shape
+    slot_block = pl.BlockSpec(
+        (fields, 1, rows, levels, width),
+        lambda i, *scalars: (0, chosen_slot(i, *scalars, rows), 0, 0, 0),
+    )
     return pl.pallas_call(
         main_kernel,
-        in_specs=vmem(7) + smem(3),
-        out_specs=vmem(2),
+        grid_spec=pltpu.PrefetchScalarGridSpec(
+            num_scalar_prefetch=3,
+            grid=(2,),
+            in_specs=[slot_block, slot_block] + vmem(5),
+            out_specs=[slot_block, pl.BlockSpec((8, LANES), lambda i, *scalars: (0, 0))],
+        ),
         out_shape=[
             jax.ShapeDtypeStruct(state.shape, F32),
             jax.ShapeDtypeStruct((8, LANES), F32),
         ],
+        input_output_aliases={4: 0},
         compiler_params=pltpu.CompilerParams(vmem_limit_bytes=VMEM_LIMIT),
         cost_estimate=pl.CostEstimate(
-            flops=12 * mine.shape[0] * 2 * KCUT * width, bytes_accessed=10**7, transcendentals=0
+            flops=12 * mine.shape[0] * 2 * KCUT * width,
+            bytes_accessed=6 * 10**6,
+            transcendentals=0,
         ),
         name="main",
-    )(state, tend, mine, away, *inverse, turn, place, block, cutoff)
+    )(place, block, cutoff, state, base, mine, away, *inverse, turn)
 
 
 def unpack(ref, base, stride, put, fields, width):
@@ -466,7 +493,7 @@
                 def put(f, start, stop, tile, i=i, side=side):
                     faces_ref[i, side, f, :, start:stop] = tile
 
-                unpack(got_ref, 64 * i + 32 * side, 128, put, fields, width)
+                unpack(got_ref, 64 * i + 32 * side, BACK, put, fields, width)
     else:
         faces_ref[...] = got_ref[...]
     turn = turn_ref[place_ref[0]]
@@ -529,7 +556,7 @@
             old = main_ref[f, rest, 0, :, start:stop]
             out_ref[f, rest, 0, :, start:stop] = old + tile * sign
 
-        unpack(back_ref, 32 * side, 64, put, fields, width)
+        unpack(back_ref, 128 + 32 * side, BACK, put, fields, width)
     else:
         out_ref[:, rest, 0] = main_ref[:, rest, 0] + back_ref[side] * sign
     cuts = [cutoff_ref[block_ref[slot] * rows + row] for slot in (mine, other)]
@@ -600,18 +627,16 @@
     west, east = edges(state, courant_x)
     west = lax.ppermute(west, "lon", [(i, (i + 1) % lon) for i in range(lon)])
     east = lax.ppermute(east, "lon", [((i + 1) % lon, i) for i in range(lon)])
-    tend, mine, other = local_tendency(
+    base, mine, other = local_tendency(
         state, courant_x, courant_y, west, east, forward, *tables
     )
     total, away = lon_sum(mine, other)
-    main, token = main_part(state, tend, total, away, inverse, *tables)
+    main, token = main_part(state, base, total, away, inverse, *tables)
 
     if packed:
-        pair, rest = faces_of_pieces(got, slots, cutoff)
-        pair, rest = (
-            lax.all_to_all(x.reshape(lat, -1, LANES), "lat", 0, 0, tiled=True).reshape(-1, LANES)
-            for x in (pair, rest)
-        )
+        back = faces_of_pieces(got, slots, cutoff).reshape(lat, BACK, LANES)
+        back = lax.all_to_all(back, "lat", 0, 0, tiled=True).reshape(lat * BACK, LANES)
+        pair = rest = back
     else:
         faces = exchange_faces(state, courant_y, face_source)
         picked = pick_slots(block_of_slot, cutoff, rows)

time: 82.9 us -> 77.5 us (0.935)
  starting transfers between devices: 24.5 us -> 19.3 us
  waiting for transfers between devices: 20.5 us -> 24.8 us
  Pallas kernels: 31.2 us -> 29.2 us
  local copies, waits for them, and re-layouts: 2.65 us -> 1.17 us
  other arithmetic: 3.39 us -> 2.46 us
    all_to_all x2 -> x1, starting transfers between devices: 12 us -> 5.99 us  [shards(): lax.all_to_all(back, 'lat', 0, 0, tiled=True).reshape(lat * BACK, LANES)]
    all_to_all x2 -> x1, waiting for transfers between devices: 2.14 us -> 4.54 us  [shards(): lax.all_to_all(back, 'lat', 0, 0, tiled=True).reshape(lat * BACK, LANES)]
    ppermute x6, waiting for transfers between devices: 16.8 us -> 18.7 us  [swap(): return lax.ppermute(array, 'lon', [(i, i ^ bit) for i in range(size)])]
    unnamed x28 -> x22, local copies, waits for them, and re-layouts: 2.65 us -> 1.17 us
    pallas_call x1, Pallas kernels: 2.56 us -> 1.38 us  [rim_spectra(): pl.pallas_call(functools.partial(rim_kernel, got.ndim == 2), in_specs=vme...]
    add x2, other arithmetic: 1.9 us -> 0.97 us  [lon_sum(): total = mine + swap(other, 1)]
    pallas_call x3, Pallas kernels: 21.2 us -> 20.3 us  [the longest x1 11.8 us: local_tendency(): pl.pallas_call(tendency_kernel, in_specs=vmem(8) + smem(3), out_specs=[pl...]
  transfers between devices with their start and end apart: 11 -> 10, of which waited for: 6 -> 8; matrix products, arithmetic and copies ran while one was open for 4% -> 3% of each run, Pallas kernels for 29% -> 30%
where the time goes in v1:
time: 77.5 us; the launch traced here: 77 us
  Pallas kernels  29.2 us (38%)
  waiting for transfers between devices  24.8 us (32%)
  starting transfers between devices  19.3 us (25%)
  other arithmetic  2.46 us (3%)
  local copies, waits for them, and re-layouts  1.17 us (2%)
    ppermute x6, waiting for transfers between devices, swap(): return lax.ppermute(array, 'lon', [(i, i ^ bit) for i in range(size)])  18.7 us
    pallas_call x1, Pallas kernels, local_tendency(): pl.pallas_call(tendency_kernel, in_specs=vmem(8) + smem(3), out_specs=[pl...  11.8 us
    all_to_all x1, starting transfers between devices, shards(): got = lax.all_to_all(sent, 'lat', 0, 0, tiled=True)  7.28 us
    all_to_all x1, starting transfers between devices, shards(): lax.all_to_all(back, 'lat', 0, 0, tiled=True).reshape(lat * BACK, LANES)  5.99 us
    pallas_call x1, Pallas kernels, main_part(): pl.pallas_call(main_kernel, grid_spec=pltpu.PrefetchScalarGridSpec(num_sc...  5.11 us
    all_to_all x1, waiting for transfers between devices, shards(): lax.all_to_all(back, 'lat', 0, 0, tiled=True).reshape(lat * BACK, LANES)  4.54 us
    ppermute x6, starting transfers between devices, swap(): return lax.ppermute(array, 'lon', [(i, i ^ bit) for i in range(size)])  4.26 us
    pallas_call x1, Pallas kernels, faces_of_pieces(): pl.pallas_call(face_kernel, in_specs=vmem(1) + smem(1), out_specs=vmem(1)...  3.47 us
  transfers between devices with their start and end apart: 10, of which 8 were waited for; matrix products, arithmetic and copies ran while one was open for 3% of the time, Pallas kernels for 30%

profile of v1, /device:TPU:0, one launch (start us, length us, event | category | flops | bytes accessed | tf_op | source)
XLA Modules:
  0.0 77.0 jit_solution(5164435266730421774)
XLA Ops:
  0.0 2.2 %pack.1 = f32[1600,128]{1,0:T(8,128)} custom-call(f32[5,3,8,8,720]{4,3,2,1,0:T(8,128)} %last_ref.1, f32[5,3,8,8,720]{4,3,2,1,0:T(8,128)} %last_ref.1, f32[3,8,8,720]{3,2,1,0:T(8,128)} %wind_ref.3, s32[3]{0:T(128)} %block_ref.7), custom_call_target="tpu_custom_call" | custom-call | flops 100000 | bytes 1700000 | tf_op jit(solution)/shard_map/pack/pallas_call | solution.py:163
  2.2 7.3 %all-to-all-start = ((f32[8,200,128]{2,1,0:T(8,128)}), f32[8,200,128]{2,1,0:T(8,128)}, u32[]{:S(2)}, u32[]{:S(2)}) async-start(f32[8,200,128]{2,1,0:T(8,128)} %bitcast.7), calls=%async_computation | async-start | bytes 1638400 | tf_op jit(solution)/shard_map/all_to_all | solution.py:625
  9.5 0.0 copy-start.3
  9.5 0.0 copy-start.5
  9.5 0.0 copy-start.7
  9.6 2.4 %edges.1 = (f32[3,8,128]{2,1,0:T(8,128)}, f32[3,8,128]{2,1,0:T(8,128)}) custom-call(f32[5,3,8,8,720]{4,3,2,1,0:T(8,128)} %last_ref.1, f32[5,3,8,8,720]{4,3,2,1,0:T(8,128)} %last_ref.1, f32[3,8,8,720]{3,2,1,0:T(8,128)} %cx_ref.1), custom_call_target="tpu_custom_call" | custom-call | flops 100000 | bytes 1200000 | tf_op jit(solution)/shard_map/edges/pallas_call | solution.py:107
  12.0 1.7 %collective-permute-start.1 = (f32[3,8,128]{2,1,0:T(8,128)}, f32[3,8,128]{2,1,0:T(8,128)S(1)}, u32[]{:S(2)}, u32[]{:S(2)}) collective-permute-start(f32[3,8,128]{2,1,0:T(8,128)} %get-tuple-element.16), channel_id=1, source_target_pairs={{1,0},{2,1},{3,2},{0,3},{5,4},{6,5},{7,6},{4,7},{9,8},{10,9},{11,1... | collective-permute-start | bytes 36872 | tf_op jit(solution)/shard_map/ppermute | solution.py:629
  13.7 0.1 pad_add_fusion.place_ref
  13.8 1.5 %collective-permute-done.west_ref = f32[3,8,128]{2,1,0:T(8,128)S(1)} collective-permute-done((f32[3,8,128]{2,1,0:T(8,128)}, f32[3,8,128]{2,1,0:T(8,128)S(1)}, u32[]{:S(2)}, u32[]{:S(2)}) %collective-permute-start) | collective-permute-done | bytes 12320 | tf_op jit(solution)/shard_map/ppermute | solution.py:628
  15.3 0.0 collective-permute-done.1.east_ref
  15.4 11.8 %tendency.1 = (f32[5,3,8,8,720]{4,3,2,1,0:T(8,128)}, f32[320,512]{1,0:T(8,128)S(1)}, f32[320,512]{1,0:T(8,128)S(1)}) custom-call(f32[5,3,8,8,720]{4,3,2,1,0:T(8,128)} %last_ref.1, f32[3,8,8,720]{3,2,1,0:T(8,128)S(1)} %copy-done.5, f32[3,8,8,720]{3,2,1,0:T(8,128)S(1)} %copy-done.6, f32[3,8,128]{2,1,0:T(8,128)S(1)} %collective-permute-done.west_ref, ...), custom_call_target="tpu_custom_call" | custom-call | flops 1415577600 | bytes 9000000 | tf_op jit(solution)/shard_map/tendency/pallas_call | solution.py:381
  27.1 2.0 %collective-permute-start.2 = (f32[320,512]{1,0:T(8,128)S(1)}, f32[320,512]{1,0:T(8,128)S(1)}, u32[]{:S(2)}, u32[]{:S(2)}) collective-permute-start(f32[320,512]{1,0:T(8,128)S(1)} %get-tuple-element.19), channel_id=1, source_target_pairs={{0,1},{1,0},{2,3},{3,2},{4,5},{5,4},{6,7},{7,6},{8,9},{9,8},{10,11... | collective-permute-start | bytes 1966088 | tf_op jit(solution)/shard_map/ppermute | solution.py:601
  29.2 1.7 %collective-permute-done.2 = f32[320,512]{1,0:T(8,128)S(1)} collective-permute-done((f32[320,512]{1,0:T(8,128)S(1)}, f32[320,512]{1,0:T(8,128)S(1)}, u32[]{:S(2)}, u32[]{:S(2)}) %collective-permute-start.2) | collective-permute-done | bytes 655392 | tf_op jit(solution)/shard_map/ppermute | solution.py:601
  30.9 0.9 %add.17 = f32[320,512]{1,0:T(8,128)} add(f32[320,512]{1,0:T(8,128)S(1)} %get-tuple-element.18, f32[320,512]{1,0:T(8,128)S(1)} %collective-permute-done.2) | non-fusion elementwise | flops 163840 | bytes 1966080 | tf_op jit(solution)/shard_map/add | solution.py:605
  31.9 0.5 collective-permute-start.3
  32.4 3.5 %faces.1 = f32[8,3,2,32,128]{4,3,2,1,0:T(8,128)} custom-call(f32[8,200,128]{2,1,0:T(8,128)} %all-to-all-done.got_ref, s32[192]{0:T(256)} %cutoff_ref.7), custom_call_target="tpu_custom_call" | custom-call | flops 100000 | bytes 1600000 | tf_op jit(solution)/shard_map/faces/pallas_call | solution.py:225
  35.9 6.0 %all-to-all-start.1 = ((f32[8,192,128]{2,1,0:T(8,128)}), f32[8,192,128]{2,1,0:T(8,128)S(1)}, u32[]{:S(2)}, u32[]{:S(2)}) async-start(f32[8,192,128]{2,1,0:T(8,128)} %bitcast.8), calls=%async_computation.1 | async-start | bytes 1572864 | tf_op jit(solution)/shard_map/all_to_all | solution.py:638
  41.9 7.3 %collective-permute-done.3 = f32[320,512]{1,0:T(8,128)} collective-permute-done((f32[320,512]{1,0:T(8,128)}, f32[320,512]{1,0:T(8,128)}, u32[]{:S(2)}, u32[]{:S(2)}) %collective-permute-start.3) | collective-permute-done | bytes 655392 | tf_op jit(solution)/shard_map/ppermute | solution.py:601
  49.2 1.4 %add.18.mine_ref = f32[320,512]{1,0:T(8,128)S(1)} add(f32[320,512]{1,0:T(8,128)} %add.17, f32[320,512]{1,0:T(8,128)} %collective-permute-done.3) | non-fusion elementwise | flops 163840 | bytes 1966080 | tf_op jit(solution)/shard_map/add | solution.py:608
  50.6 0.1 collective-permute-start.4
  50.7 2.1 %collective-permute-done.4.away_ref = f32[320,512]{1,0:T(8,128)S(1)} collective-permute-done((f32[320,512]{1,0:T(8,128)S(1)}, f32[320,512]{1,0:T(8,128)S(1)}, u32[]{:S(2)}, u32[]{:S(2)}) %collective-permute-start.4) | collective-permute-done | bytes 655392 | tf_op jit(solution)/shard_map/ppermute | solution.py:601
  52.7 5.1 %main.1 = (f32[5,3,8,8,720]{4,3,2,1,0:T(8,128)}, f32[8,128]{1,0:T(8,128)S(1)}) custom-call(s32[2]{0:T(128)S(1)} %pad_add_fusion.place_ref, s32[3]{0:T(128)S(1)} %copy-done.10, s32[192]{0:T(256)S(1)} %copy-done.9, f32[5,3,8,8,720]{4,3,2,1,0:T(8,128)} %last_ref.1, f32[5,3,8,8,720]{4,3,2,1,0:T(8,128)} %get-tuple-element.17.base_ref, ...), custom_call_target="tpu_custom_call", output_to_operand_aliasing={{0}: (4, {})} | custom-call | flops 1415577600 | bytes 6000000 | tf_op jit(solution)/shard_map/main/pallas_call | solution.py:444
  57.9 4.5 %all-to-all-done.1 = f32[8,192,128]{2,1,0:T(8,128)S(1)} async-done(((f32[8,192,128]{2,1,0:T(8,128)}), f32[8,192,128]{2,1,0:T(8,128)S(1)}, u32[]{:S(2)}, u32[]{:S(2)}) %all-to-all-start.1) | async-done | bytes 786464 | tf_op jit(solution)/shard_map/all_to_all | solution.py:638
  62.4 1.1 %copy-done.4 = bf16[720,512]{1,0:T(8,128)(2,1)S(1)} copy-done((bf16[720,512]{1,0:T(8,128)(2,1)S(1)}, bf16[720,512]{1,0:T(8,128)(2,1)}, u32[]{:S(2)}) %copy-start.4) | copy-done | bytes 737304
  63.5 1.4 %rim_spectra.1 = (f32[2,2,5,8,720]{4,3,2,1,0:T(8,128)S(1)}, f32[80,512]{1,0:T(8,128)S(1)}, f32[80,512]{1,0:T(8,128)S(1)}) custom-call(f32[8,128]{1,0:T(8,128)S(1)} %get-tuple-element.21.token_ref, f32[1536,128]{1,0:T(8,128)S(1)} %bitcast.5, bf16[720,512]{1,0:T(8,128)(2,1)S(1)} %copy-done.2, bf16[720,512]{1,0:T(8,128)(2,1)S(1)} %copy-done.4, ...), custom_call_target="tpu_custom_call" | custom-call | flops 353894400 | bytes 3000000 | tf_op jit(solution)/shard_map/rim_spectra/pallas_call | solution.py:512
  64.9 0.1 collective-permute-start.5
  65.0 1.4 %collective-permute-done.5 = f32[80,512]{1,0:T(8,128)S(1)} collective-permute-done((f32[80,512]{1,0:T(8,128)S(1)}, f32[80,512]{1,0:T(8,128)S(1)}, u32[]{:S(2)}, u32[]{:S(2)}) %collective-permute-start.5) | collective-permute-done | bytes 163872 | tf_op jit(solution)/shard_map/ppermute | solution.py:601
  66.4 1.5 %collective-permute-start.6 = (f32[80,512]{1,0:T(8,128)S(1)}, f32[80,512]{1,0:T(8,128)S(1)}, u32[]{:S(2)}, u32[]{:S(2)}) collective-permute-start(f32[80,512]{1,0:T(8,128)S(1)} %add.19), channel_id=1, source_target_pairs={{0,2},{1,3},{2,0},{3,1},{4,6},{5,7},{6,4},{7,5},{8,10},{9,11},{10,... | collective-permute-start | bytes 491528 | tf_op jit(solution)/shard_map/ppermute | solution.py:601
  67.8 4.9 %collective-permute-done.6 = f32[80,512]{1,0:T(8,128)S(1)} collective-permute-done((f32[80,512]{1,0:T(8,128)S(1)}, f32[80,512]{1,0:T(8,128)S(1)}, u32[]{:S(2)}, u32[]{:S(2)}) %collective-permute-start.6) | collective-permute-done | bytes 163872 | tf_op jit(solution)/shard_map/ppermute | solution.py:601
  72.7 0.1 collective-permute-start.7
  72.8 1.4 %collective-permute-done.7.away_ref = f32[80,512]{1,0:T(8,128)S(1)} collective-permute-done((f32[80,512]{1,0:T(8,128)S(1)}, f32[80,512]{1,0:T(8,128)S(1)}, u32[]{:S(2)}, u32[]{:S(2)}) %collective-permute-start.7) | collective-permute-done | bytes 163872 | tf_op jit(solution)/shard_map/ppermute | solution.py:601
  74.2 2.8 %final.1 = f32[5,3,8,8,720]{4,3,2,1,0:T(8,128)} custom-call(f32[5,3,8,8,720]{4,3,2,1,0:T(8,128)} %get-tuple-element.20.main_ref, f32[2,2,5,8,720]{4,3,2,1,0:T(8,128)S(1)} %get-tuple-element.22.pair_ref, f32[1536,128]{1,0:T(8,128)S(1)} %bitcast.6, f32[80,512]{1,0:T(8,128)S(1)} %add.20.mine_ref, ...), custom_call_target="tpu_custom_call", output_to_operand_aliasing={{}: (0, {})} | custom-call | flops 353894400 | bytes 4000000 | tf_op jit(solution)/shard_map/final/pallas_call | solution.py:582
  (22 shorter events, 0.1 us)
Async XLA Ops:
  2.2 30.2 %all-to-all-start = ((f32[8,200,128]{2,1,0:T(8,128)}), f32[8,200,128]{2,1,0:T(8,128)}, u32[]{:S(2)}, u32[]{:S(2)}) async-start(f32[8,200,128]{2,1,0:T(8,128)} %bitcast.7), calls=%async_computation | async-start | bytes 1638400 | tf_op jit(solution)/shard_map/all_to_all | solution.py:625
  9.5 5.8 %copy-start.2 = (bf16[720,512]{1,0:T(8,128)(2,1)S(1)}, bf16[720,512]{1,0:T(8,128)(2,1)}, u32[]{:S(2)}) copy-start(bf16[720,512]{1,0:T(8,128)(2,1)} %constant.27.clone.high_ref) | copy-start | bytes 2211844
  9.5 5.8 %copy-start.3 = (bf16[720,512]{1,0:T(8,128)(2,1)S(1)}, bf16[720,512]{1,0:T(8,128)(2,1)}, u32[]{:S(2)}) copy-start(bf16[720,512]{1,0:T(8,128)(2,1)} %constant.28.clone.low_ref) | copy-start | bytes 2211844
  9.5 5.8 %copy-start.5 = (f32[3,8,8,720]{3,2,1,0:T(8,128)S(1)}, f32[3,8,8,720]{3,2,1,0:T(8,128)}, u32[]{:S(2)}) copy-start(f32[3,8,8,720]{3,2,1,0:T(8,128)} %cx_ref.1) | copy-start | bytes 1658884
  9.5 5.8 %copy-start.6 = (f32[3,8,8,720]{3,2,1,0:T(8,128)S(1)}, f32[3,8,8,720]{3,2,1,0:T(8,128)}, u32[]{:S(2)}) copy-start(f32[3,8,8,720]{3,2,1,0:T(8,128)} %wind_ref.3) | copy-start | bytes 1658884
  9.5 5.8 %copy-start.7 = (f32[4,1,512]{2,1,0:T(1,128)S(1)}, f32[4,1,512]{2,1,0:T(1,128)}, u32[]{:S(2)}) copy-start(f32[4,1,512]{2,1,0:T(1,128)} %constant.31.clone.turn_ref) | copy-start | bytes 24580
  9.5 5.8 %copy-start.8 = (s32[192]{0:T(256)S(1)}, s32[192]{0:T(256)}, u32[]{:S(2)}) copy-start(s32[192]{0:T(256)} %cutoff_ref.7) | copy-start | bytes 2308
  9.6 5.8 %copy-start.10 = (s32[3]{0:T(128)S(1)}, s32[3]{0:T(128)}, u32[]{:S(2)}) copy-start(s32[3]{0:T(128)} %block_ref.7) | copy-start | bytes 40
  12.0 3.3 %collective-permute-start = (f32[3,8,128]{2,1,0:T(8,128)}, f32[3,8,128]{2,1,0:T(8,128)S(1)}, u32[]{:S(2)}, u32[]{:S(2)}) collective-permute-start(f32[3,8,128]{2,1,0:T(8,128)} %get-tuple-element.15), channel_id=1, source_target_pairs={{0,1},{1,2},{2,3},{3,0},{4,5},{5,6},{6,7},{7,4},{8,9},{9,10},{10,1... | collective-permute-start | bytes 36872 | tf_op jit(solution)/shard_map/ppermute | solution.py:628
  12.0 3.4 %collective-permute-start.1 = (f32[3,8,128]{2,1,0:T(8,128)}, f32[3,8,128]{2,1,0:T(8,128)S(1)}, u32[]{:S(2)}, u32[]{:S(2)}) collective-permute-start(f32[3,8,128]{2,1,0:T(8,128)} %get-tuple-element.16), channel_id=1, source_target_pairs={{1,0},{2,1},{3,2},{0,3},{5,4},{6,5},{7,6},{4,7},{9,8},{10,9},{11,1... | collective-permute-start | bytes 36872 | tf_op jit(solution)/shard_map/ppermute | solution.py:629
  27.1 3.8 %collective-permute-start.2 = (f32[320,512]{1,0:T(8,128)S(1)}, f32[320,512]{1,0:T(8,128)S(1)}, u32[]{:S(2)}, u32[]{:S(2)}) collective-permute-start(f32[320,512]{1,0:T(8,128)S(1)} %get-tuple-element.19), channel_id=1, source_target_pairs={{0,1},{1,0},{2,3},{3,2},{4,5},{5,4},{6,7},{7,6},{8,9},{9,8},{10,11... | collective-permute-start | bytes 1966088 | tf_op jit(solution)/shard_map/ppermute | solution.py:601
  31.8 20.9 %copy-start = (bf16[512,720]{1,0:T(8,128)(2,1)S(1)}, bf16[512,720]{1,0:T(8,128)(2,1)}, u32[]{:S(2)}) copy-start(bf16[512,720]{1,0:T(8,128)(2,1)} %constant.29.clone.high_ref) | copy-start | bytes 2211844
  31.8 20.9 %copy-start.1 = (bf16[512,720]{1,0:T(8,128)(2,1)S(1)}, bf16[512,720]{1,0:T(8,128)(2,1)}, u32[]{:S(2)}) copy-start(bf16[512,720]{1,0:T(8,128)(2,1)} %constant.30.clone.low_ref) | copy-start | bytes 2211844
  31.9 20.9 %copy-start.9 = (s32[192]{0:T(256)S(1)}, s32[192]{0:T(256)}, u32[]{:S(2)}) copy-start(s32[192]{0:T(256)} %cutoff_ref.7) | copy-start | bytes 2308
  31.9 17.3 %collective-permute-start.3 = (f32[320,512]{1,0:T(8,128)}, f32[320,512]{1,0:T(8,128)}, u32[]{:S(2)}, u32[]{:S(2)}) collective-permute-start(f32[320,512]{1,0:T(8,128)} %add.17), channel_id=1, source_target_pairs={{0,2},{1,3},{2,0},{3,1},{4,6},{5,7},{6,4},{7,5},{8,10},{9,11},{10,... | collective-permute-start | bytes 1966088 | tf_op jit(solution)/shard_map/ppermute | solution.py:601
  35.9 26.5 %all-to-all-start.1 = ((f32[8,192,128]{2,1,0:T(8,128)}), f32[8,192,128]{2,1,0:T(8,128)S(1)}, u32[]{:S(2)}, u32[]{:S(2)}) async-start(f32[8,192,128]{2,1,0:T(8,128)} %bitcast.8), calls=%async_computation.1 | async-start | bytes 1572864 | tf_op jit(solution)/shard_map/all_to_all | solution.py:638
  50.6 2.2 %collective-permute-start.4 = (f32[320,512]{1,0:T(8,128)S(1)}, f32[320,512]{1,0:T(8,128)S(1)}, u32[]{:S(2)}, u32[]{:S(2)}) collective-permute-start(f32[320,512]{1,0:T(8,128)S(1)} %add.18.mine_ref), channel_id=1, source_target_pairs={{0,1},{1,0},{2,3},{3,2},{4,5},{5,4},{6,7},{7,6},{8,9},{9,8},{10,11... | collective-permute-start | bytes 1966088 | tf_op jit(solution)/shard_map/ppermute | solution.py:601
  62.4 1.1 %copy-start.4 = (bf16[720,512]{1,0:T(8,128)(2,1)S(1)}, bf16[720,512]{1,0:T(8,128)(2,1)}, u32[]{:S(2)}) copy-start(bf16[720,512]{1,0:T(8,128)(2,1)} %constant.28.clone.low_ref) | copy-start | bytes 2211844
  64.9 1.5 %collective-permute-start.5 = (f32[80,512]{1,0:T(8,128)S(1)}, f32[80,512]{1,0:T(8,128)S(1)}, u32[]{:S(2)}, u32[]{:S(2)}) collective-permute-start(f32[80,512]{1,0:T(8,128)S(1)} %get-tuple-element.24), channel_id=1, source_target_pairs={{0,1},{1,0},{2,3},{3,2},{4,5},{5,4},{6,7},{7,6},{8,9},{9,8},{10,11... | collective-permute-start | bytes 491528 | tf_op jit(solution)/shard_map/ppermute | solution.py:601
  66.4 6.3 %collective-permute-start.6 = (f32[80,512]{1,0:T(8,128)S(1)}, f32[80,512]{1,0:T(8,128)S(1)}, u32[]{:S(2)}, u32[]{:S(2)}) collective-permute-start(f32[80,512]{1,0:T(8,128)S(1)} %add.19), channel_id=1, source_target_pairs={{0,2},{1,3},{2,0},{3,1},{4,6},{5,7},{6,4},{7,5},{8,10},{9,11},{10,... | collective-permute-start | bytes 491528 | tf_op jit(solution)/shard_map/ppermute | solution.py:601
  72.7 1.5 %collective-permute-start.7 = (f32[80,512]{1,0:T(8,128)S(1)}, f32[80,512]{1,0:T(8,128)S(1)}, u32[]{:S(2)}, u32[]{:S(2)}) collective-permute-start(f32[80,512]{1,0:T(8,128)S(1)} %add.20.mine_ref), channel_id=1, source_target_pairs={{0,1},{1,0},{2,3},{3,2},{4,5},{5,4},{6,7},{7,6},{8,9},{9,8},{10,11... | collective-permute-start | bytes 491528 | tf_op jit(solution)/shard_map/ppermute | solution.py:601

commit v2 on v1

--- a/solution.py
+++ b/solution.py
@@ -12,7 +12,7 @@
 NLON = 2880
 KCUT = 256
 LANES = 128
-VMEM_LIMIT = 50 * 1024 * 1024
+MIB = 1024 * 1024
 BF16 = jnp.bfloat16
 F32 = jnp.float32
 
@@ -176,7 +176,10 @@
     )(state, state, courant_y, block)
 
 
-def face_kernel(got_ref, cutoff_ref, out_ref, face_ref, table_ref, slot_ref, sem):
+def face_kernel(
+    got_ref, cutoff_ref, later_in_ref, out_ref, later_ref, face_ref, table_ref, slot_ref, sem
+):
+    del later_in_ref, later_ref
     parts = got_ref.shape[0]
     slots = face_ref.shape[0] // parts
     count = parts * slots
@@ -220,13 +223,17 @@
             out[1] = face_ref[slots * d + slot]
 
 
-def faces_of_pieces(got, slots, cutoff):
+def faces_of_pieces(got, slots, cutoff, later):
     parts = got.shape[0]
     return pl.pallas_call(
         face_kernel,
-        in_specs=vmem(1) + smem(1),
-        out_specs=vmem(1)[0],
-        out_shape=jax.ShapeDtypeStruct((parts, slots, 2, 32, LANES), F32),
+        in_specs=vmem(1) + smem(1) + [pl.BlockSpec(memory_space=pl.ANY)],
+        out_specs=vmem(1) + [pl.BlockSpec(memory_space=pl.ANY)],
+        out_shape=[
+            jax.ShapeDtypeStruct((parts, slots, 2, 32, LANES), F32),
+            jax.ShapeDtypeStruct(later.shape, F32),
+        ],
+        input_output_aliases={2: 1},
         scratch_shapes=[
             pltpu.VMEM((parts * slots, 32, LANES), F32),
             pltpu.SMEM((parts, 8, LANES), F32),
@@ -235,7 +242,7 @@
         ],
         cost_estimate=pl.CostEstimate(flops=10**5, bytes_accessed=1600000, transcendentals=0),
         name="faces",
-    )(got, cutoff)
+    )(got, cutoff, later)
 
 
 def to_pieces(units, parts):
@@ -388,7 +395,7 @@
             pltpu.VMEM(state.shape, F32),
             pltpu.SemaphoreType.DMA((slots,)),
         ],
-        compiler_params=pltpu.CompilerParams(vmem_limit_bytes=VMEM_LIMIT),
+        compiler_params=pltpu.CompilerParams(vmem_limit_bytes=28 * MIB),
         cost_estimate=pl.CostEstimate(
             flops=6 * count * 2 * KCUT * width * 2, bytes_accessed=9 * 10**6, transcendentals=0
         ),
@@ -412,10 +419,12 @@
     high_ref,
     low_ref,
     turn_ref,
+    after_ref,
     out_ref,
     token_ref,
 ):
     fields, _, rows, levels, width = state_ref.shape
+    del after_ref
     token_ref[...] = jnp.zeros_like(token_ref)
     i = pl.program_id(0)
     turn = turn_ref[place_ref[0]]
@@ -435,7 +444,7 @@
         )
 
 
-def main_part(state, base, mine, away, inverse, turn, place, block, cutoff):
+def main_part(after, state, base, mine, away, inverse, turn, place, block, cutoff):
     fields, slots, rows, levels, width = state.shape
     slot_block = pl.BlockSpec(
         (fields, 1, rows, levels, width),
@@ -446,22 +455,22 @@
         grid_spec=pltpu.PrefetchScalarGridSpec(
             num_scalar_prefetch=3,
             grid=(2,),
-            in_specs=[slot_block, slot_block] + vmem(5),
-            out_specs=[slot_block, pl.BlockSpec((8, LANES), lambda i, *scalars: (0, 0))],
+            in_specs=[slot_block, slot_block] + vmem(6),
+            out_specs=[slot_block, pl.BlockSpec((1, 2 * KCUT), lambda i, *scalars: (0, 0))],
         ),
         out_shape=[
             jax.ShapeDtypeStruct(state.shape, F32),
-            jax.ShapeDtypeStruct((8, LANES), F32),
+            jax.ShapeDtypeStruct((1, 2 * KCUT), F32),
         ],
         input_output_aliases={4: 0},
-        compiler_params=pltpu.CompilerParams(vmem_limit_bytes=VMEM_LIMIT),
+        compiler_params=pltpu.CompilerParams(vmem_limit_bytes=28 * MIB),
         cost_estimate=pl.CostEstimate(
             flops=12 * mine.shape[0] * 2 * KCUT * width,
             bytes_accessed=6 * 10**6,
             transcendentals=0,
         ),
         name="main",
-    )(place, block, cutoff, state, base, mine, away, *inverse, turn)
+    )(place, block, cutoff, state, base, mine, away, *inverse, turn, after)
 
 
 def unpack(ref, base, stride, put, fields, width):
@@ -475,7 +484,6 @@
 
 def rim_kernel(
     packed,
-    token_ref,
     got_ref,
     high_ref,
     low_ref,
@@ -484,8 +492,10 @@
     faces_ref,
     mine_ref,
     other_ref,
+    token_ref,
 ):
     _, _, fields, levels, width = faces_ref.shape
+    token_ref[...] = jnp.zeros_like(token_ref)
     if packed:
         for i in range(2):
             for side in range(2):
@@ -506,22 +516,27 @@
     other_ref[...] = spec[2 * fields * levels :]
 
 
-def rim_spectra(token, got, shape, forward, turn, place):
+def rim_spectra(got, shape, forward, turn, place):
     _, _, fields, levels, width = shape
     spec = jax.ShapeDtypeStruct((2 * fields * levels, 2 * KCUT), F32)
     return pl.pallas_call(
         functools.partial(rim_kernel, got.ndim == 2),
-        in_specs=vmem(5) + smem(1),
-        out_specs=vmem(3),
-        out_shape=[jax.ShapeDtypeStruct(shape, F32), spec, spec],
-        compiler_params=pltpu.CompilerParams(vmem_limit_bytes=VMEM_LIMIT),
+        in_specs=vmem(4) + smem(1),
+        out_specs=vmem(4),
+        out_shape=[
+            jax.ShapeDtypeStruct(shape, F32),
+            spec,
+            spec,
+            jax.ShapeDtypeStruct((8, LANES), F32),
+        ],
+        compiler_params=pltpu.CompilerParams(vmem_limit_bytes=16 * MIB),
         cost_estimate=pl.CostEstimate(
             flops=24 * fields * levels * 2 * KCUT * width,
             bytes_accessed=3 * 10**6,
             transcendentals=0,
         ),
         name="rim_spectra",
-    )(token, got, *forward, turn, place)
+    )(got, *forward, turn, place)
 
 
 def final_kernel(
@@ -586,7 +601,7 @@
         out_specs=block_spec,
         out_shape=jax.ShapeDtypeStruct(main.shape, F32),
         input_output_aliases={0: 0},
-        compiler_params=pltpu.CompilerParams(vmem_limit_bytes=VMEM_LIMIT),
+        compiler_params=pltpu.CompilerParams(vmem_limit_bytes=16 * MIB),
         cost_estimate=pl.CostEstimate(
             flops=12 * mine.shape[0] * 2 * KCUT * width,
             bytes_accessed=4 * 10**6,
@@ -601,12 +616,14 @@
     return lax.ppermute(array, "lon", [(i, i ^ bit) for i in range(size)])
 
 
-def lon_sum(mine, other):
+def lon_sum(mine, other, last=None):
     total = mine + swap(other, 1)
     bit = 2
     while bit < lax.axis_size("lon"):
         total = total + swap(total, bit)
         bit *= 2
+    if last is not None:
+        total = total + last
     return total, swap(total, 1)
 
 
@@ -630,20 +647,19 @@
     base, mine, other = local_tendency(
         state, courant_x, courant_y, west, east, forward, *tables
     )
-    total, away = lon_sum(mine, other)
-    main, token = main_part(state, base, total, away, inverse, *tables)
-
     if packed:
-        back = faces_of_pieces(got, slots, cutoff).reshape(lat, BACK, LANES)
-        back = lax.all_to_all(back, "lat", 0, 0, tiled=True).reshape(lat * BACK, LANES)
-        pair = rest = back
+        back, other = faces_of_pieces(got, slots, cutoff, other)
+        back = lax.all_to_all(back.reshape(lat, BACK, LANES), "lat", 0, 0, tiled=True)
+        pair = rest = back.reshape(lat * BACK, LANES)
     else:
         faces = exchange_faces(state, courant_y, face_source)
         picked = pick_slots(block_of_slot, cutoff, rows)
         pair, rest = faces[jnp.stack(picked[:2])], faces[picked[2]]
+    total, away = lon_sum(mine, other)
     shape = (2, 2, fields, levels, width)
-    pair, rim_mine, rim_other = rim_spectra(token, pair, shape, forward, turn, place)
-    rim_total, rim_away = lon_sum(rim_mine, rim_other)
+    pair, rim_mine, rim_other, token = rim_spectra(pair, shape, forward, turn, place)
+    main, token = main_part(token, state, base, total, away, inverse, *tables)
+    rim_total, rim_away = lon_sum(rim_mine, rim_other, token)
     return final_part(main, pair, rest, rim_total, rim_away, inverse, *tables)
 
 

time: 77.5 us -> 80.9 us (1.044)
  local copies, waits for them, and re-layouts: 1.17 us -> 8.03 us
  waiting for transfers between devices: 24.8 us -> 22.2 us
  starting transfers between devices: 19.3 us -> 18.3 us
    unnamed x22 -> x32, local copies, waits for them, and re-layouts: 1.17 us -> 8.03 us
    all_to_all x1, waiting for transfers between devices: 4.54 us -> 1.65 us  [shards(): lax.all_to_all(back.reshape(lat, BACK, LANES), 'lat', 0, 0, tiled=True)]
    pallas_call x1, Pallas kernels: 11.8 us -> 10.6 us  [local_tendency(): pl.pallas_call(tendency_kernel, in_specs=vmem(8) + smem(3), out_specs=[pl...]
    ppermute x6, starting transfers between devices: 4.26 us -> 3.3 us  [swap(): return lax.ppermute(array, 'lon', [(i, i ^ bit) for i in range(size)])]
  transfers between devices with their start and end apart: 10 -> 10, of which waited for: 8 -> 6; matrix products, arithmetic and copies ran while one was open for 3% -> 3% of each run, Pallas kernels for 30% -> 25%
where the time goes in v2:
time: 80.9 us; the launch traced here: 80.3 us
  Pallas kernels  29.1 us (36%)
  waiting for transfers between devices  22.2 us (27%)
  starting transfers between devices  18.3 us (23%)
  local copies, waits for them, and re-layouts  8.03 us (10%)
  other arithmetic  2.48 us (3%)
    ppermute x6, waiting for transfers between devices, swap(): return lax.ppermute(array, 'lon', [(i, i ^ bit) for i in range(size)])  19 us
    pallas_call x1, Pallas kernels, local_tendency(): pl.pallas_call(tendency_kernel, in_specs=vmem(8) + smem(3), out_specs=[pl...  10.6 us
    unnamed x32, local copies, waits for them, and re-layouts  8.03 us
    all_to_all x1, starting transfers between devices, shards(): got = lax.all_to_all(sent, 'lat', 0, 0, tiled=True)  7.28 us
    all_to_all x1, starting transfers between devices, shards(): lax.all_to_all(back.reshape(lat, BACK, LANES), 'lat', 0, 0, tiled=True)  5.98 us
    pallas_call x1, Pallas kernels, main_part(): pl.pallas_call(main_kernel, grid_spec=pltpu.PrefetchScalarGridSpec(num_sc...  5.34 us
    pallas_call x1, Pallas kernels, faces_of_pieces(): pl.pallas_call(face_kernel, in_specs=vmem(1) + smem(1) + [pl.BlockSpec(me...  3.48 us
    ppermute x6, starting transfers between devices, swap(): return lax.ppermute(array, 'lon', [(i, i ^ bit) for i in range(size)])  3.3 us
  transfers between devices with their start and end apart: 10, of which 6 were waited for; matrix products, arithmetic and copies ran while one was open for 3% of the time, Pallas kernels for 25%

profile of v2, /device:TPU:0, one launch (start us, length us, event | category | flops | bytes accessed | tf_op | source)
XLA Modules:
  0.0 80.3 jit_solution(14009373622736172591)
XLA Ops:
  0.0 2.2 %pack.1 = f32[1600,128]{1,0:T(8,128)} custom-call(f32[5,3,8,8,720]{4,3,2,1,0:T(8,128)} %state_ref.3, f32[5,3,8,8,720]{4,3,2,1,0:T(8,128)} %state_ref.3, f32[3,8,8,720]{3,2,1,0:T(8,128)} %wind_ref.3, s32[3]{0:T(128)} %block_ref.7), custom_call_target="tpu_custom_call" | custom-call | flops 100000 | bytes 1700000 | tf_op jit(solution)/shard_map/pack/pallas_call | solution.py:163
  2.2 7.3 %all-to-all-start = ((f32[8,200,128]{2,1,0:T(8,128)}), f32[8,200,128]{2,1,0:T(8,128)}, u32[]{:S(2)}, u32[]{:S(2)}) async-start(f32[8,200,128]{2,1,0:T(8,128)} %bitcast.7), calls=%async_computation | async-start | bytes 1638400 | tf_op jit(solution)/shard_map/all_to_all | solution.py:642
  9.5 2.4 %edges.1 = (f32[3,8,128]{2,1,0:T(8,128)}, f32[3,8,128]{2,1,0:T(8,128)}) custom-call(f32[5,3,8,8,720]{4,3,2,1,0:T(8,128)} %state_ref.3, f32[5,3,8,8,720]{4,3,2,1,0:T(8,128)} %state_ref.3, f32[3,8,8,720]{3,2,1,0:T(8,128)} %cx_ref.1), custom_call_target="tpu_custom_call" | custom-call | flops 100000 | bytes 1200000 | tf_op jit(solution)/shard_map/edges/pallas_call | solution.py:107
  11.9 1.7 %collective-permute-start.1 = (f32[3,8,128]{2,1,0:T(8,128)}, f32[3,8,128]{2,1,0:T(8,128)}, u32[]{:S(2)}, u32[]{:S(2)}) collective-permute-start(f32[3,8,128]{2,1,0:T(8,128)} %get-tuple-element.19), channel_id=1, source_target_pairs={{1,0},{2,1},{3,2},{0,3},{5,4},{6,5},{7,6},{4,7},{9,8},{10,9},{11,1... | collective-permute-start | bytes 36872 | tf_op jit(solution)/shard_map/ppermute | solution.py:646
  13.6 0.1 pad_add_fusion.place_ref
  13.7 1.6 %collective-permute-done.west_ref = f32[3,8,128]{2,1,0:T(8,128)} collective-permute-done((f32[3,8,128]{2,1,0:T(8,128)}, f32[3,8,128]{2,1,0:T(8,128)}, u32[]{:S(2)}, u32[]{:S(2)}) %collective-permute-start) | collective-permute-done | bytes 12320 | tf_op jit(solution)/shard_map/ppermute | solution.py:645
  15.4 1.1 %copy-done.3 = bf16[720,512]{1,0:T(8,128)(2,1)S(1)} copy-done((bf16[720,512]{1,0:T(8,128)(2,1)S(1)}, bf16[720,512]{1,0:T(8,128)(2,1)}, u32[]{:S(2)}) %copy-start.3) | copy-done | bytes 737304
  16.5 1.1 %copy-done.5 = bf16[720,512]{1,0:T(8,128)(2,1)S(1)} copy-done((bf16[720,512]{1,0:T(8,128)(2,1)S(1)}, bf16[720,512]{1,0:T(8,128)(2,1)}, u32[]{:S(2)}) %copy-start.5) | copy-done | bytes 737304
  17.6 1.1 %copy-done.8 = f32[3,8,8,720]{3,2,1,0:T(8,128)S(1)} copy-done((f32[3,8,8,720]{3,2,1,0:T(8,128)S(1)}, f32[3,8,8,720]{3,2,1,0:T(8,128)}, u32[]{:S(2)}) %copy-start.8) | copy-done | bytes 552984
  18.6 0.7 copy-done.14
  19.3 10.6 %tendency.1 = (f32[5,3,8,8,720]{4,3,2,1,0:T(8,128)}, f32[320,512]{1,0:T(8,128)S(1)}, f32[320,512]{1,0:T(8,128)S(1)}) custom-call(f32[5,3,8,8,720]{4,3,2,1,0:T(8,128)S(1)} %copy-done, f32[3,8,8,720]{3,2,1,0:T(8,128)S(1)} %copy-done.7, f32[3,8,8,720]{3,2,1,0:T(8,128)S(1)} %copy-done.8, f32[3,8,128]{2,1,0:T(8,128)} %collective-permute-done.west_ref, ...), custom_call_target="tpu_custom_call" | custom-call | flops 1415577600 | bytes 9000000 | tf_op jit(solution)/shard_map/tendency/pallas_call | solution.py:388
  30.0 0.8 %copy-done.9 = f32[320,512]{1,0:T(8,128)} copy-done((f32[320,512]{1,0:T(8,128)}, f32[320,512]{1,0:T(8,128)S(1)}, u32[]{:S(2)}) %copy-start.9) | copy-done | bytes 655384
  30.8 0.9 %copy-done.10 = f32[320,512]{1,0:T(8,128)} copy-done((f32[320,512]{1,0:T(8,128)}, f32[320,512]{1,0:T(8,128)S(1)}, u32[]{:S(2)}) %copy-start.10) | copy-done | bytes 655384
  31.6 3.5 %faces.1 = (f32[8,3,2,32,128]{4,3,2,1,0:T(8,128)}, f32[320,512]{1,0:T(8,128)}) custom-call(f32[8,200,128]{2,1,0:T(8,128)} %all-to-all-done.got_ref, s32[192]{0:T(256)} %cutoff_ref.7, f32[320,512]{1,0:T(8,128)} %copy-done.9), custom_call_target="tpu_custom_call", output_to_operand_aliasing={{1}: (2, {})} | custom-call | flops 100000 | bytes 1600000 | tf_op jit(solution)/shard_map/faces/pallas_call | solution.py:228
  35.1 2.0 %collective-permute-start.2 = (f32[320,512]{1,0:T(8,128)}, f32[320,512]{1,0:T(8,128)}, u32[]{:S(2)}, u32[]{:S(2)}) collective-permute-start(f32[320,512]{1,0:T(8,128)} %get-tuple-element.23), channel_id=1, source_target_pairs={{0,1},{1,0},{2,3},{3,2},{4,5},{5,4},{6,7},{7,6},{8,9},{9,8},{10,11... | collective-permute-start | bytes 1966088 | tf_op jit(solution)/shard_map/ppermute | solution.py:616
  37.1 6.0 %all-to-all-start.1 = ((f32[8,192,128]{2,1,0:T(8,128)}), f32[8,192,128]{2,1,0:T(8,128)}, u32[]{:S(2)}, u32[]{:S(2)}) async-start(f32[8,192,128]{2,1,0:T(8,128)} %bitcast.8), calls=%async_computation.1 | async-start | bytes 1572864 | tf_op jit(solution)/shard_map/all_to_all | solution.py:652
  43.1 1.4 %add.27 = f32[320,512]{1,0:T(8,128)S(1)} add(f32[320,512]{1,0:T(8,128)} %copy-done.10, f32[320,512]{1,0:T(8,128)} %collective-permute-done.2) | non-fusion elementwise | flops 163840 | bytes 1966080 | tf_op jit(solution)/shard_map/add | solution.py:620
  44.5 0.6 collective-permute-start.3
  45.1 15.8 %collective-permute-done.3 = f32[320,512]{1,0:T(8,128)S(1)} collective-permute-done((f32[320,512]{1,0:T(8,128)S(1)}, f32[320,512]{1,0:T(8,128)S(1)}, u32[]{:S(2)}, u32[]{:S(2)}) %collective-permute-start.3) | collective-permute-done | bytes 655392 | tf_op jit(solution)/shard_map/ppermute | solution.py:616
  61.0 1.0 %add.28.mine_ref = f32[320,512]{1,0:T(8,128)} add(f32[320,512]{1,0:T(8,128)S(1)} %add.27, f32[320,512]{1,0:T(8,128)S(1)} %collective-permute-done.3) | non-fusion elementwise | flops 163840 | bytes 1966080 | tf_op jit(solution)/shard_map/add | solution.py:623
  61.9 1.7 %all-to-all-done.1 = f32[8,192,128]{2,1,0:T(8,128)} async-done(((f32[8,192,128]{2,1,0:T(8,128)}), f32[8,192,128]{2,1,0:T(8,128)}, u32[]{:S(2)}, u32[]{:S(2)}) %all-to-all-start.1) | async-done | bytes 786464 | tf_op jit(solution)/shard_map/all_to_all | solution.py:652
  63.6 1.2 %copy-done.4 = bf16[720,512]{1,0:T(8,128)(2,1)S(1)} copy-done((bf16[720,512]{1,0:T(8,128)(2,1)S(1)}, bf16[720,512]{1,0:T(8,128)(2,1)}, u32[]{:S(2)}) %copy-start.4) | copy-done | bytes 737304
  64.8 1.1 %copy-done.6 = bf16[720,512]{1,0:T(8,128)(2,1)S(1)} copy-done((bf16[720,512]{1,0:T(8,128)(2,1)S(1)}, bf16[720,512]{1,0:T(8,128)(2,1)}, u32[]{:S(2)}) %copy-start.6) | copy-done | bytes 737304
  65.9 2.0 %rim_spectra.1 = (f32[2,2,5,8,720]{4,3,2,1,0:T(8,128)S(1)}, f32[80,512]{1,0:T(8,128)S(1)}, f32[80,512]{1,0:T(8,128)S(1)}, f32[8,128]{1,0:T(8,128)S(1)}) custom-call(f32[1536,128]{1,0:T(8,128)} %bitcast.4.got_ref.back_ref, bf16[720,512]{1,0:T(8,128)(2,1)S(1)} %copy-done.6, bf16[720,512]{1,0:T(8,128)(2,1)S(1)} %copy-done.4, f32[4,1,512]{2,1,0:T(1,128)S(1)} %copy-done.11, ...), custom_call_target="tpu_custom_call" | custom-call | flops 353894400 | bytes 3000000 | tf_op jit(solution)/shard_map/rim_spectra/pallas_call | solution.py:522
  67.9 0.1 collective-permute-start.5
  68.0 1.4 %collective-permute-done.5 = f32[80,512]{1,0:T(8,128)S(1)} collective-permute-done((f32[80,512]{1,0:T(8,128)S(1)}, f32[80,512]{1,0:T(8,128)S(1)}, u32[]{:S(2)}, u32[]{:S(2)}) %collective-permute-start.5) | collective-permute-done | bytes 163872 | tf_op jit(solution)/shard_map/ppermute | solution.py:616
  69.4 0.6 collective-permute-start.6
  70.0 5.3 %main.1 = (f32[5,3,8,8,720]{4,3,2,1,0:T(8,128)}, f32[1,512]{1,0:T(1,128)S(1)}) custom-call(s32[2]{0:T(128)S(1)} %pad_add_fusion.place_ref, s32[3]{0:T(128)S(1)} %copy-done.15, s32[192]{0:T(256)S(1)} %copy-done.13, f32[5,3,8,8,720]{4,3,2,1,0:T(8,128)S(1)} %copy-done, ...), custom_call_target="tpu_custom_call", output_to_operand_aliasing={{0}: (4, {})} | custom-call | flops 1415577600 | bytes 6000000 | tf_op jit(solution)/shard_map/main/pallas_call | solution.py:453
  75.4 0.3 collective-permute-done.6
  75.7 0.1 collective-permute-start.7
  75.8 1.4 %collective-permute-done.7.away_ref = f32[80,512]{1,0:T(8,128)S(1)} collective-permute-done((f32[80,512]{1,0:T(8,128)S(1)}, f32[80,512]{1,0:T(8,128)S(1)}, u32[]{:S(2)}, u32[]{:S(2)}) %collective-permute-start.7) | collective-permute-done | bytes 163872 | tf_op jit(solution)/shard_map/ppermute | solution.py:616
  77.2 3.1 %final.1 = f32[5,3,8,8,720]{4,3,2,1,0:T(8,128)} custom-call(f32[5,3,8,8,720]{4,3,2,1,0:T(8,128)} %get-tuple-element.26.main_ref, f32[2,2,5,8,720]{4,3,2,1,0:T(8,128)S(1)} %get-tuple-element.27.pair_ref, f32[1536,128]{1,0:T(8,128)} %bitcast.4.got_ref.back_ref, f32[80,512]{1,0:T(8,128)S(1)} %add_add_fusion.mine_ref, ...), custom_call_target="tpu_custom_call", output_to_operand_aliasing={{}: (0, {})} | custom-call | flops 353894400 | bytes 4000000 | tf_op jit(solution)/shard_map/final/pallas_call | solution.py:597
  (32 shorter events, 0.1 us)
Async XLA Ops:
  2.2 29.5 %all-to-all-start = ((f32[8,200,128]{2,1,0:T(8,128)}), f32[8,200,128]{2,1,0:T(8,128)}, u32[]{:S(2)}, u32[]{:S(2)}) async-start(f32[8,200,128]{2,1,0:T(8,128)} %bitcast.7), calls=%async_computation | async-start | bytes 1638400 | tf_op jit(solution)/shard_map/all_to_all | solution.py:642
  9.5 5.9 %copy-start = (f32[5,3,8,8,720]{4,3,2,1,0:T(8,128)S(1)}, f32[5,3,8,8,720]{4,3,2,1,0:T(8,128)}, u32[]{:S(2)}) copy-start(f32[5,3,8,8,720]{4,3,2,1,0:T(8,128)} %state_ref.3) | copy-start | bytes 8294404
  9.5 5.9 %copy-start.7 = (f32[3,8,8,720]{3,2,1,0:T(8,128)S(1)}, f32[3,8,8,720]{3,2,1,0:T(8,128)}, u32[]{:S(2)}) copy-start(f32[3,8,8,720]{3,2,1,0:T(8,128)} %cx_ref.1) | copy-start | bytes 1658884
  9.5 5.9 %copy-start.11 = (f32[4,1,512]{2,1,0:T(1,128)S(1)}, f32[4,1,512]{2,1,0:T(1,128)}, u32[]{:S(2)}) copy-start(f32[4,1,512]{2,1,0:T(1,128)} %constant.31.clone.turn_ref) | copy-start | bytes 24580
  9.5 5.9 %copy-start.12 = (s32[192]{0:T(256)S(1)}, s32[192]{0:T(256)}, u32[]{:S(2)}) copy-start(s32[192]{0:T(256)} %cutoff_ref.7) | copy-start | bytes 2308
  11.9 3.4 %collective-permute-start = (f32[3,8,128]{2,1,0:T(8,128)}, f32[3,8,128]{2,1,0:T(8,128)}, u32[]{:S(2)}, u32[]{:S(2)}) collective-permute-start(f32[3,8,128]{2,1,0:T(8,128)} %get-tuple-element.18), channel_id=1, source_target_pairs={{0,1},{1,2},{2,3},{3,0},{4,5},{5,6},{6,7},{7,4},{8,9},{9,10},{10,1... | collective-permute-start | bytes 36872 | tf_op jit(solution)/shard_map/ppermute | solution.py:645
  11.9 3.4 %collective-permute-start.1 = (f32[3,8,128]{2,1,0:T(8,128)}, f32[3,8,128]{2,1,0:T(8,128)}, u32[]{:S(2)}, u32[]{:S(2)}) collective-permute-start(f32[3,8,128]{2,1,0:T(8,128)} %get-tuple-element.19), channel_id=1, source_target_pairs={{1,0},{2,1},{3,2},{0,3},{5,4},{6,5},{7,6},{4,7},{9,8},{10,9},{11,1... | collective-permute-start | bytes 36872 | tf_op jit(solution)/shard_map/ppermute | solution.py:646
  15.3 1.1 %copy-start.3 = (bf16[720,512]{1,0:T(8,128)(2,1)S(1)}, bf16[720,512]{1,0:T(8,128)(2,1)}, u32[]{:S(2)}) copy-start(bf16[720,512]{1,0:T(8,128)(2,1)} %constant.28.clone.low_ref) | copy-start | bytes 2211844
  16.5 1.1 %copy-start.5 = (bf16[720,512]{1,0:T(8,128)(2,1)S(1)}, bf16[720,512]{1,0:T(8,128)(2,1)}, u32[]{:S(2)}) copy-start(bf16[720,512]{1,0:T(8,128)(2,1)} %constant.27.clone.high_ref) | copy-start | bytes 2211844
  17.6 1.1 %copy-start.8 = (f32[3,8,8,720]{3,2,1,0:T(8,128)S(1)}, f32[3,8,8,720]{3,2,1,0:T(8,128)}, u32[]{:S(2)}) copy-start(f32[3,8,8,720]{3,2,1,0:T(8,128)} %wind_ref.3) | copy-start | bytes 1658884
  18.6 0.7 copy-start.14
  29.9 0.8 %copy-start.9 = (f32[320,512]{1,0:T(8,128)}, f32[320,512]{1,0:T(8,128)S(1)}, u32[]{:S(2)}) copy-start(f32[320,512]{1,0:T(8,128)S(1)} %get-tuple-element.22.later_in_ref) | copy-start | bytes 1966084
  30.8 0.9 %copy-start.10 = (f32[320,512]{1,0:T(8,128)}, f32[320,512]{1,0:T(8,128)S(1)}, u32[]{:S(2)}) copy-start(f32[320,512]{1,0:T(8,128)S(1)} %get-tuple-element.21) | copy-start | bytes 1966084
  35.1 7.9 %collective-permute-start.2 = (f32[320,512]{1,0:T(8,128)}, f32[320,512]{1,0:T(8,128)}, u32[]{:S(2)}, u32[]{:S(2)}) collective-permute-start(f32[320,512]{1,0:T(8,128)} %get-tuple-element.23), channel_id=1, source_target_pairs={{0,1},{1,0},{2,3},{3,2},{4,5},{5,4},{6,7},{7,6},{8,9},{9,8},{10,11... | collective-permute-start | bytes 1966088 | tf_op jit(solution)/shard_map/ppermute | solution.py:616
  37.1 26.5 %all-to-all-start.1 = ((f32[8,192,128]{2,1,0:T(8,128)}), f32[8,192,128]{2,1,0:T(8,128)}, u32[]{:S(2)}, u32[]{:S(2)}) async-start(f32[8,192,128]{2,1,0:T(8,128)} %bitcast.8), calls=%async_computation.1 | async-start | bytes 1572864 | tf_op jit(solution)/shard_map/all_to_all | solution.py:652
  43.1 26.9 %copy-start.13 = (s32[192]{0:T(256)S(1)}, s32[192]{0:T(256)}, u32[]{:S(2)}) copy-start(s32[192]{0:T(256)} %cutoff_ref.7) | copy-start | bytes 2308
  43.1 26.9 %copy-start.15 = (s32[3]{0:T(128)S(1)}, s32[3]{0:T(128)}, u32[]{:S(2)}) copy-start(s32[3]{0:T(128)} %block_ref.7) | copy-start | bytes 40
  44.5 16.4 %collective-permute-start.3 = (f32[320,512]{1,0:T(8,128)S(1)}, f32[320,512]{1,0:T(8,128)S(1)}, u32[]{:S(2)}, u32[]{:S(2)}) collective-permute-start(f32[320,512]{1,0:T(8,128)S(1)} %add.27), channel_id=1, source_target_pairs={{0,2},{1,3},{2,0},{3,1},{4,6},{5,7},{6,4},{7,5},{8,10},{9,11},{10,... | collective-permute-start | bytes 1966088 | tf_op jit(solution)/shard_map/ppermute | solution.py:616
  61.9 8.1 %collective-permute-start.4 = (f32[320,512]{1,0:T(8,128)}, f32[320,512]{1,0:T(8,128)}, u32[]{:S(2)}, u32[]{:S(2)}) collective-permute-start(f32[320,512]{1,0:T(8,128)} %add.28.mine_ref), channel_id=1, source_target_pairs={{0,1},{1,0},{2,3},{3,2},{4,5},{5,4},{6,7},{7,6},{8,9},{9,8},{10,11... | collective-permute-start | bytes 1966088 | tf_op jit(solution)/shard_map/ppermute | solution.py:616
  63.6 6.4 %copy-start.1 = (bf16[512,720]{1,0:T(8,128)(2,1)S(1)}, bf16[512,720]{1,0:T(8,128)(2,1)}, u32[]{:S(2)}) copy-start(bf16[512,720]{1,0:T(8,128)(2,1)} %constant.30.clone.low_ref) | copy-start | bytes 2211844
  63.6 6.5 %copy-start.2 = (bf16[512,720]{1,0:T(8,128)(2,1)S(1)}, bf16[512,720]{1,0:T(8,128)(2,1)}, u32[]{:S(2)}) copy-start(bf16[512,720]{1,0:T(8,128)(2,1)} %constant.29.clone.high_ref) | copy-start | bytes 2211844
  63.6 1.2 %copy-start.4 = (bf16[720,512]{1,0:T(8,128)(2,1)S(1)}, bf16[720,512]{1,0:T(8,128)(2,1)}, u32[]{:S(2)}) copy-start(bf16[720,512]{1,0:T(8,128)(2,1)} %constant.28.clone.low_ref) | copy-start | bytes 2211844
  64.8 1.1 %copy-start.6 = (bf16[720,512]{1,0:T(8,128)(2,1)S(1)}, bf16[720,512]{1,0:T(8,128)(2,1)}, u32[]{:S(2)}) copy-start(bf16[720,512]{1,0:T(8,128)(2,1)} %constant.27.clone.high_ref) | copy-start | bytes 2211844
  67.9 1.5 %collective-permute-start.5 = (f32[80,512]{1,0:T(8,128)S(1)}, f32[80,512]{1,0:T(8,128)S(1)}, u32[]{:S(2)}, u32[]{:S(2)}) collective-permute-start(f32[80,512]{1,0:T(8,128)S(1)} %get-tuple-element.29), channel_id=1, source_target_pairs={{0,1},{1,0},{2,3},{3,2},{4,5},{5,4},{6,7},{7,6},{8,9},{9,8},{10,11... | collective-permute-start | bytes 491528 | tf_op jit(solution)/shard_map/ppermute | solution.py:616
  69.4 6.3 %collective-permute-start.6 = (f32[80,512]{1,0:T(8,128)S(1)}, f32[80,512]{1,0:T(8,128)S(1)}, u32[]{:S(2)}, u32[]{:S(2)}) collective-permute-start(f32[80,512]{1,0:T(8,128)S(1)} %add.29), channel_id=1, source_target_pairs={{0,2},{1,3},{2,0},{3,1},{4,6},{5,7},{6,4},{7,5},{8,10},{9,11},{10,... | collective-permute-start | bytes 491528 | tf_op jit(solution)/shard_map/ppermute | solution.py:616
  75.7 1.5 %collective-permute-start.7 = (f32[80,512]{1,0:T(8,128)S(1)}, f32[80,512]{1,0:T(8,128)S(1)}, u32[]{:S(2)}, u32[]{:S(2)}) collective-permute-start(f32[80,512]{1,0:T(8,128)S(1)} %add_add_fusion.mine_ref), channel_id=1, source_target_pairs={{0,1},{1,0},{2,3},{3,2},{4,5},{5,4},{6,7},{7,6},{8,9},{9,8},{10,11... | collective-permute-start | bytes 491528 | tf_op jit(solution)/shard_map/ppermute | solution.py:616

commit v3 on v2

--- a/solution.py
+++ b/solution.py
@@ -395,7 +395,7 @@
             pltpu.VMEM(state.shape, F32),
             pltpu.SemaphoreType.DMA((slots,)),
         ],
-        compiler_params=pltpu.CompilerParams(vmem_limit_bytes=28 * MIB),
+        compiler_params=pltpu.CompilerParams(vmem_limit_bytes=58 * MIB),
         cost_estimate=pl.CostEstimate(
             flops=6 * count * 2 * KCUT * width * 2, bytes_accessed=9 * 10**6, transcendentals=0
         ),
@@ -463,7 +463,7 @@
             jax.ShapeDtypeStruct((1, 2 * KCUT), F32),
         ],
         input_output_aliases={4: 0},
-        compiler_params=pltpu.CompilerParams(vmem_limit_bytes=28 * MIB),
+        compiler_params=pltpu.CompilerParams(vmem_limit_bytes=58 * MIB),
         cost_estimate=pl.CostEstimate(
             flops=12 * mine.shape[0] * 2 * KCUT * width,
             bytes_accessed=6 * 10**6,
@@ -529,7 +529,7 @@
             spec,
             jax.ShapeDtypeStruct((8, LANES), F32),
         ],
-        compiler_params=pltpu.CompilerParams(vmem_limit_bytes=16 * MIB),
+        compiler_params=pltpu.CompilerParams(vmem_limit_bytes=58 * MIB),
         cost_estimate=pl.CostEstimate(
             flops=24 * fields * levels * 2 * KCUT * width,
             bytes_accessed=3 * 10**6,
@@ -601,7 +601,7 @@
         out_specs=block_spec,
         out_shape=jax.ShapeDtypeStruct(main.shape, F32),
         input_output_aliases={0: 0},
-        compiler_params=pltpu.CompilerParams(vmem_limit_bytes=16 * MIB),
+        compiler_params=pltpu.CompilerParams(vmem_limit_bytes=58 * MIB),
         cost_estimate=pl.CostEstimate(
             flops=12 * mine.shape[0] * 2 * KCUT * width,
             bytes_accessed=4 * 10**6,

time: 80.9 us -> 83.3 us (1.030)
  Pallas kernels: 29.1 us -> 34.5 us
  local copies, waits for them, and re-layouts: 8.03 us -> 4.49 us
  waiting for transfers between devices: 22.2 us -> 24 us
  starting transfers between devices: 18.3 us -> 17.3 us
    unnamed x32 -> x18, local copies, waits for them, and re-layouts: 8.03 us -> 4.49 us
    pallas_call x1, Pallas kernels: 10.6 us -> 13.6 us  [local_tendency(): pl.pallas_call(tendency_kernel, in_specs=vmem(8) + smem(3), out_specs=[pl...]
    all_to_all x1, waiting for transfers between devices: 1.65 us -> 3.6 us  [shards(): lax.all_to_all(back.reshape(lat, BACK, LANES), 'lat', 0, 0, tiled=True)]
    pallas_call x1, Pallas kernels: 1.97 us -> 3.14 us  [rim_spectra(): pl.pallas_call(functools.partial(rim_kernel, got.ndim == 2), in_specs=vme...]
    ppermute x6, starting transfers between devices: 3.3 us -> 2.24 us  [swap(): return lax.ppermute(array, 'lon', [(i, i ^ bit) for i in range(size)])]
    add x1, other arithmetic: 0.95 us -> 0.11 us  [lon_sum(): total = total + swap(total, bit)]
  transfers between devices with their start and end apart: 10 -> 10, of which waited for: 6 -> 6; matrix products, arithmetic and copies ran while one was open for 3% -> 2% of each run, Pallas kernels for 25% -> 30%
where the time goes in v3:
time: 83.3 us; the launch traced here: 82.8 us
  Pallas kernels  34.5 us (41%)
  waiting for transfers between devices  24 us (29%)
  starting transfers between devices  17.3 us (21%)
  local copies, waits for them, and re-layouts  4.49 us (5%)
  other arithmetic  2.49 us (3%)
    ppermute x6, waiting for transfers between devices, swap(): return lax.ppermute(array, 'lon', [(i, i ^ bit) for i in range(size)])  18.8 us
    pallas_call x1, Pallas kernels, local_tendency(): pl.pallas_call(tendency_kernel, in_specs=vmem(8) + smem(3), out_specs=[pl...  13.6 us
    all_to_all x1, starting transfers between devices, shards(): got = lax.all_to_all(sent, 'lat', 0, 0, tiled=True)  7.28 us
    pallas_call x1, Pallas kernels, main_part(): pl.pallas_call(main_kernel, grid_spec=pltpu.PrefetchScalarGridSpec(num_sc...  6.15 us
    all_to_all x1, starting transfers between devices, shards(): lax.all_to_all(back.reshape(lat, BACK, LANES), 'lat', 0, 0, tiled=True)  6 us
    unnamed x18, local copies, waits for them, and re-layouts  4.49 us
    pallas_call x1, Pallas kernels, final_part(): pl.pallas_call(functools.partial(final_kernel, back.ndim == 2), grid=(2,)...  3.83 us
    all_to_all x1, waiting for transfers between devices, shards(): lax.all_to_all(back.reshape(lat, BACK, LANES), 'lat', 0, 0, tiled=True)  3.6 us
  transfers between devices with their start and end apart: 10, of which 6 were waited for; matrix products, arithmetic and copies ran while one was open for 2% of the time, Pallas kernels for 30%

profile of v3, /device:TPU:0, one launch (start us, length us, event | category | flops | bytes accessed | tf_op | source)
XLA Modules:
  0.0 82.8 jit_solution(14543686808247681253)
XLA Ops:
  0.0 2.1 %pack.1 = f32[1600,128]{1,0:T(8,128)} custom-call(f32[5,3,8,8,720]{4,3,2,1,0:T(8,128)} %state_ref.3, f32[5,3,8,8,720]{4,3,2,1,0:T(8,128)} %state_ref.3, f32[3,8,8,720]{3,2,1,0:T(8,128)} %wind_ref.3, s32[3]{0:T(128)} %block_ref.7), custom_call_target="tpu_custom_call" | custom-call | flops 100000 | bytes 1700000 | tf_op jit(solution)/shard_map/pack/pallas_call | solution.py:163
  2.1 7.3 %all-to-all-start = ((f32[8,200,128]{2,1,0:T(8,128)}), f32[8,200,128]{2,1,0:T(8,128)S(1)}, u32[]{:S(2)}, u32[]{:S(2)}) async-start(f32[8,200,128]{2,1,0:T(8,128)} %bitcast.8), calls=%async_computation | async-start | bytes 1638400 | tf_op jit(solution)/shard_map/all_to_all | solution.py:642
  9.4 2.2 %edges.1 = (f32[3,8,128]{2,1,0:T(8,128)}, f32[3,8,128]{2,1,0:T(8,128)}) custom-call(f32[5,3,8,8,720]{4,3,2,1,0:T(8,128)} %state_ref.3, f32[5,3,8,8,720]{4,3,2,1,0:T(8,128)} %state_ref.3, f32[3,8,8,720]{3,2,1,0:T(8,128)} %cx_ref.1), custom_call_target="tpu_custom_call" | custom-call | flops 100000 | bytes 1200000 | tf_op jit(solution)/shard_map/edges/pallas_call | solution.py:107
  11.7 1.7 %collective-permute-start.1 = (f32[3,8,128]{2,1,0:T(8,128)}, f32[3,8,128]{2,1,0:T(8,128)S(1)}, u32[]{:S(2)}, u32[]{:S(2)}) collective-permute-start(f32[3,8,128]{2,1,0:T(8,128)} %get-tuple-element.19), channel_id=1, source_target_pairs={{1,0},{2,1},{3,2},{0,3},{5,4},{6,5},{7,6},{4,7},{9,8},{10,9},{11,1... | collective-permute-start | bytes 36872 | tf_op jit(solution)/shard_map/ppermute | solution.py:646
  13.4 0.6 pad_add_fusion.place_ref
  14.0 0.9 %collective-permute-done.west_ref = f32[3,8,128]{2,1,0:T(8,128)S(1)} collective-permute-done((f32[3,8,128]{2,1,0:T(8,128)}, f32[3,8,128]{2,1,0:T(8,128)S(1)}, u32[]{:S(2)}, u32[]{:S(2)}) %collective-permute-start) | collective-permute-done | bytes 12320 | tf_op jit(solution)/shard_map/ppermute | solution.py:645
  15.0 0.6 copy-done.7
  15.6 0.6 copy-done.8
  16.2 13.6 %tendency.1 = (f32[5,3,8,8,720]{4,3,2,1,0:T(8,128)}, f32[320,512]{1,0:T(8,128)}, f32[320,512]{1,0:T(8,128)}) custom-call(f32[5,3,8,8,720]{4,3,2,1,0:T(8,128)} %state_ref.3, f32[3,8,8,720]{3,2,1,0:T(8,128)} %cx_ref.1, f32[3,8,8,720]{3,2,1,0:T(8,128)} %wind_ref.3, f32[3,8,128]{2,1,0:T(8,128)} %copy-done.7, f32[3,8,128]{2,1,0:T(8,128)} %copy-done.8, ...), custom_call_target="tpu_custom_call" | custom-call | flops 1415577600 | bytes 9000000 | tf_op jit(solution)/shard_map/tendency/pallas_call | solution.py:388
  29.7 0.6 all-to-all-done.got_ref
  30.3 0.9 %copy-done.1 = f32[8,200,128]{2,1,0:T(8,128)} copy-done((f32[8,200,128]{2,1,0:T(8,128)}, f32[8,200,128]{2,1,0:T(8,128)S(1)}, u32[]{:S(2)}) %copy-start.1) | copy-done | bytes 819224
  31.2 3.5 %faces.1 = (f32[8,3,2,32,128]{4,3,2,1,0:T(8,128)}, f32[320,512]{1,0:T(8,128)}) custom-call(f32[8,200,128]{2,1,0:T(8,128)} %copy-done.1, s32[192]{0:T(256)} %cutoff_ref.7, f32[320,512]{1,0:T(8,128)} %get-tuple-element.22.later_in_ref), custom_call_target="tpu_custom_call", output_to_operand_aliasing={{1}: (2, {})} | custom-call | flops 100000 | bytes 1600000 | tf_op jit(solution)/shard_map/faces/pallas_call | solution.py:228
  34.7 0.8 collective-permute-start.2
  35.5 6.0 %all-to-all-start.1 = ((f32[8,192,128]{2,1,0:T(8,128)}), f32[8,192,128]{2,1,0:T(8,128)S(1)}, u32[]{:S(2)}, u32[]{:S(2)}) async-start(f32[8,192,128]{2,1,0:T(8,128)} %bitcast.9), calls=%async_computation.1 | async-start | bytes 1572864 | tf_op jit(solution)/shard_map/all_to_all | solution.py:652
  41.5 0.1 add.27
  41.6 0.6 collective-permute-start.3
  42.2 15.8 %collective-permute-done.3 = f32[320,512]{1,0:T(8,128)S(1)} collective-permute-done((f32[320,512]{1,0:T(8,128)S(1)}, f32[320,512]{1,0:T(8,128)S(1)}, u32[]{:S(2)}, u32[]{:S(2)}) %collective-permute-start.3) | collective-permute-done | bytes 655392 | tf_op jit(solution)/shard_map/ppermute | solution.py:616
  58.1 0.1 add.28.mine_ref
  58.2 0.1 collective-permute-start.4
  58.3 3.6 %all-to-all-done.1 = f32[8,192,128]{2,1,0:T(8,128)S(1)} async-done(((f32[8,192,128]{2,1,0:T(8,128)}), f32[8,192,128]{2,1,0:T(8,128)S(1)}, u32[]{:S(2)}, u32[]{:S(2)}) %all-to-all-start.1) | async-done | bytes 786464 | tf_op jit(solution)/shard_map/all_to_all | solution.py:652
  61.9 0.9 %copy-done = f32[8,192,128]{2,1,0:T(8,128)} copy-done((f32[8,192,128]{2,1,0:T(8,128)}, f32[8,192,128]{2,1,0:T(8,128)S(1)}, u32[]{:S(2)}) %copy-start) | copy-done | bytes 786456
  62.8 3.1 %rim_spectra.1 = (f32[2,2,5,8,720]{4,3,2,1,0:T(8,128)}, f32[80,512]{1,0:T(8,128)}, f32[80,512]{1,0:T(8,128)}, f32[8,128]{1,0:T(8,128)}) custom-call(f32[1536,128]{1,0:T(8,128)} %bitcast.6, bf16[720,512]{1,0:T(8,128)(2,1)} %constant.27.clone.high_ref, bf16[720,512]{1,0:T(8,128)(2,1)} %constant.28.clone.low_ref, f32[4,1,512]{2,1,0:T(1,128)} %constant.31.clone.turn_ref, ...), custom_call_target="tpu_custom_call" | custom-call | flops 353894400 | bytes 3000000 | tf_op jit(solution)/shard_map/rim_spectra/pallas_call | solution.py:522
  65.9 1.6 %collective-permute-done.5 = f32[80,512]{1,0:T(8,128)S(1)} collective-permute-done((f32[80,512]{1,0:T(8,128)}, f32[80,512]{1,0:T(8,128)S(1)}, u32[]{:S(2)}, u32[]{:S(2)}) %collective-permute-start.5) | collective-permute-done | bytes 163872 | tf_op jit(solution)/shard_map/ppermute | solution.py:616
  67.5 0.9 %add.29 = f32[80,512]{1,0:T(8,128)S(1)} add(f32[80,512]{1,0:T(8,128)} %get-tuple-element.28, f32[80,512]{1,0:T(8,128)S(1)} %collective-permute-done.5) | non-fusion elementwise | flops 40960 | bytes 491520 | tf_op jit(solution)/shard_map/add | solution.py:620
  68.5 0.7 collective-permute-start.6
  69.2 0.9 %copy-done.4 = f32[320,512]{1,0:T(8,128)} copy-done((f32[320,512]{1,0:T(8,128)}, f32[320,512]{1,0:T(8,128)S(1)}, u32[]{:S(2)}) %copy-start.4) | copy-done | bytes 655384
  70.0 6.1 %main.1 = (f32[5,3,8,8,720]{4,3,2,1,0:T(8,128)}, f32[1,512]{1,0:T(1,128)}) custom-call(s32[2]{0:T(128)} %pad_add_fusion.place_ref, s32[3]{0:T(128)} %block_ref.7, s32[192]{0:T(256)} %cutoff_ref.7, f32[5,3,8,8,720]{4,3,2,1,0:T(8,128)} %state_ref.3, f32[5,3,8,8,720]{4,3,2,1,0:T(8,128)} %get-tuple-element.20.base_ref, ...), custom_call_target="tpu_custom_call", output_to_operand_aliasing={{0}: (4, {})} | custom-call | flops 1415577600 | bytes 6000000 | tf_op jit(solution)/shard_map/main/pallas_call | solution.py:453
  76.2 0.7 add_add_fusion.mine_ref
  76.9 0.1 collective-permute-start.7
  77.0 1.4 %collective-permute-done.7.away_ref = f32[80,512]{1,0:T(8,128)S(1)} collective-permute-done((f32[80,512]{1,0:T(8,128)S(1)}, f32[80,512]{1,0:T(8,128)S(1)}, u32[]{:S(2)}, u32[]{:S(2)}) %collective-permute-start.7) | collective-permute-done | bytes 163872 | tf_op jit(solution)/shard_map/ppermute | solution.py:616
  78.3 0.7 copy-done.6
  79.0 3.8 %final.1 = f32[5,3,8,8,720]{4,3,2,1,0:T(8,128)} custom-call(f32[5,3,8,8,720]{4,3,2,1,0:T(8,128)} %get-tuple-element.26.main_ref, f32[2,2,5,8,720]{4,3,2,1,0:T(8,128)} %get-tuple-element.27.pair_ref, f32[1536,128]{1,0:T(8,128)} %bitcast.7, f32[80,512]{1,0:T(8,128)} %copy-done.5, f32[80,512]{1,0:T(8,128)} %copy-done.6, ...), custom_call_target="tpu_custom_call", output_to_operand_aliasing={{}: (0, {})} | custom-call | flops 353894400 | bytes 4000000 | tf_op jit(solution)/shard_map/final/pallas_call | solution.py:597
  (18 shorter events, 0.1 us)
Async XLA Ops:
  2.1 28.2 %all-to-all-start = ((f32[8,200,128]{2,1,0:T(8,128)}), f32[8,200,128]{2,1,0:T(8,128)S(1)}, u32[]{:S(2)}, u32[]{:S(2)}) async-start(f32[8,200,128]{2,1,0:T(8,128)} %bitcast.8), calls=%async_computation | async-start | bytes 1638400 | tf_op jit(solution)/shard_map/all_to_all | solution.py:642
  11.7 3.3 %collective-permute-start = (f32[3,8,128]{2,1,0:T(8,128)}, f32[3,8,128]{2,1,0:T(8,128)S(1)}, u32[]{:S(2)}, u32[]{:S(2)}) collective-permute-start(f32[3,8,128]{2,1,0:T(8,128)} %get-tuple-element.18), channel_id=1, source_target_pairs={{0,1},{1,2},{2,3},{3,0},{4,5},{5,6},{6,7},{7,4},{8,9},{9,10},{10,1... | collective-permute-start | bytes 36872 | tf_op jit(solution)/shard_map/ppermute | solution.py:645
  11.7 3.4 %collective-permute-start.1 = (f32[3,8,128]{2,1,0:T(8,128)}, f32[3,8,128]{2,1,0:T(8,128)S(1)}, u32[]{:S(2)}, u32[]{:S(2)}) collective-permute-start(f32[3,8,128]{2,1,0:T(8,128)} %get-tuple-element.19), channel_id=1, source_target_pairs={{1,0},{2,1},{3,2},{0,3},{5,4},{6,5},{7,6},{4,7},{9,8},{10,9},{11,1... | collective-permute-start | bytes 36872 | tf_op jit(solution)/shard_map/ppermute | solution.py:646
  15.0 0.6 copy-start.7
  15.6 0.6 copy-start.8
  29.7 11.8 %copy-start.3 = (f32[320,512]{1,0:T(8,128)S(1)}, f32[320,512]{1,0:T(8,128)}, u32[]{:S(2)}) copy-start(f32[320,512]{1,0:T(8,128)} %get-tuple-element.21) | copy-start | bytes 1966084
  30.3 0.9 %copy-start.1 = (f32[8,200,128]{2,1,0:T(8,128)}, f32[8,200,128]{2,1,0:T(8,128)S(1)}, u32[]{:S(2)}) copy-start(f32[8,200,128]{2,1,0:T(8,128)S(1)} %all-to-all-done.got_ref) | copy-start | bytes 2457604
  34.7 6.8 %collective-permute-start.2 = (f32[320,512]{1,0:T(8,128)}, f32[320,512]{1,0:T(8,128)S(1)}, u32[]{:S(2)}, u32[]{:S(2)}) collective-permute-start(f32[320,512]{1,0:T(8,128)} %get-tuple-element.23), channel_id=1, source_target_pairs={{0,1},{1,0},{2,3},{3,2},{4,5},{5,4},{6,7},{7,6},{8,9},{9,8},{10,11... | collective-permute-start | bytes 1966088 | tf_op jit(solution)/shard_map/ppermute | solution.py:616
  35.5 26.4 %all-to-all-start.1 = ((f32[8,192,128]{2,1,0:T(8,128)}), f32[8,192,128]{2,1,0:T(8,128)S(1)}, u32[]{:S(2)}, u32[]{:S(2)}) async-start(f32[8,192,128]{2,1,0:T(8,128)} %bitcast.9), calls=%async_computation.1 | async-start | bytes 1572864 | tf_op jit(solution)/shard_map/all_to_all | solution.py:652
  41.6 16.4 %collective-permute-start.3 = (f32[320,512]{1,0:T(8,128)S(1)}, f32[320,512]{1,0:T(8,128)S(1)}, u32[]{:S(2)}, u32[]{:S(2)}) collective-permute-start(f32[320,512]{1,0:T(8,128)S(1)} %add.27), channel_id=1, source_target_pairs={{0,2},{1,3},{2,0},{3,1},{4,6},{5,7},{6,4},{7,5},{8,10},{9,11},{10,... | collective-permute-start | bytes 1966088 | tf_op jit(solution)/shard_map/ppermute | solution.py:616
  58.2 11.0 %copy-start.2 = (f32[320,512]{1,0:T(8,128)}, f32[320,512]{1,0:T(8,128)S(1)}, u32[]{:S(2)}) copy-start(f32[320,512]{1,0:T(8,128)S(1)} %add.28.mine_ref) | copy-start | bytes 1966084
  58.2 10.9 %collective-permute-start.4 = (f32[320,512]{1,0:T(8,128)S(1)}, f32[320,512]{1,0:T(8,128)S(1)}, u32[]{:S(2)}, u32[]{:S(2)}) collective-permute-start(f32[320,512]{1,0:T(8,128)S(1)} %add.28.mine_ref), channel_id=1, source_target_pairs={{0,1},{1,0},{2,3},{3,2},{4,5},{5,4},{6,7},{7,6},{8,9},{9,8},{10,11... | collective-permute-start | bytes 1966088 | tf_op jit(solution)/shard_map/ppermute | solution.py:616
  61.9 0.9 %copy-start = (f32[8,192,128]{2,1,0:T(8,128)}, f32[8,192,128]{2,1,0:T(8,128)S(1)}, u32[]{:S(2)}) copy-start(f32[8,192,128]{2,1,0:T(8,128)S(1)} %all-to-all-done.1) | copy-start | bytes 2359300
  65.9 1.6 %collective-permute-start.5 = (f32[80,512]{1,0:T(8,128)}, f32[80,512]{1,0:T(8,128)S(1)}, u32[]{:S(2)}, u32[]{:S(2)}) collective-permute-start(f32[80,512]{1,0:T(8,128)} %get-tuple-element.29), channel_id=1, source_target_pairs={{0,1},{1,0},{2,3},{3,2},{4,5},{5,4},{6,7},{7,6},{8,9},{9,8},{10,11... | collective-permute-start | bytes 491528 | tf_op jit(solution)/shard_map/ppermute | solution.py:616
  68.5 7.7 %collective-permute-start.6 = (f32[80,512]{1,0:T(8,128)S(1)}, f32[80,512]{1,0:T(8,128)S(1)}, u32[]{:S(2)}, u32[]{:S(2)}) collective-permute-start(f32[80,512]{1,0:T(8,128)S(1)} %add.29), channel_id=1, source_target_pairs={{0,2},{1,3},{2,0},{3,1},{4,6},{5,7},{6,4},{7,5},{8,10},{9,11},{10,... | collective-permute-start | bytes 491528 | tf_op jit(solution)/shard_map/ppermute | solution.py:616
  69.2 0.9 %copy-start.4 = (f32[320,512]{1,0:T(8,128)}, f32[320,512]{1,0:T(8,128)S(1)}, u32[]{:S(2)}) copy-start(f32[320,512]{1,0:T(8,128)S(1)} %collective-permute-done.4.away_ref) | copy-start | bytes 1966084
  76.9 1.5 %copy-start.5 = (f32[80,512]{1,0:T(8,128)}, f32[80,512]{1,0:T(8,128)S(1)}, u32[]{:S(2)}) copy-start(f32[80,512]{1,0:T(8,128)S(1)} %add_add_fusion.mine_ref) | copy-start | bytes 491524
  76.9 1.5 %collective-permute-start.7 = (f32[80,512]{1,0:T(8,128)S(1)}, f32[80,512]{1,0:T(8,128)S(1)}, u32[]{:S(2)}, u32[]{:S(2)}) collective-permute-start(f32[80,512]{1,0:T(8,128)S(1)} %add_add_fusion.mine_ref), channel_id=1, source_target_pairs={{0,1},{1,0},{2,3},{3,2},{4,5},{5,4},{6,7},{7,6},{8,9},{9,8},{10,11... | collective-permute-start | bytes 491528 | tf_op jit(solution)/shard_map/ppermute | solution.py:616
  78.3 0.7 copy-start.6
